TPU v7x, 512 devices: a whole 4x8x8 slice. The times are simulated.
512 devices in a mesh: inst: 64 (over y_lo, x, z), tp: 8 (over y_hi, core).
Axes of the slice: x: 4, y: 8 (y_hi: 4, y_lo: 2; y = y_hi * 2 + y_lo), z: 8, core: 2. Of those that a mesh axis runs over, the one named last changes fastest.
Arguments:
- queries: bfloat16 [512, 8192], P('inst', 'tp'), as said below
- new_kv: bfloat16 [512, 2048], P('inst', 'tp'), may hold values from -6 to 6
- cache: bfloat16 [512, 1024, 2048], P('inst', None, 'tp'), as said below
- lengths: int32 [512], P('inst'), may hold values from 128 to 1024, as said below
- migrate_slot: int32 [64], P('inst'), may hold values from 0 to 7
- pool: bfloat16 [512, 128, 2048], P('inst', None, 'tp'), may hold values from -6 to 6
- prefix_blocks: int32 [512, 16], P('inst'), may hold values from -1 to 511, as said below
Outputs:
- attended: bfloat16 [512, 8192], P(('inst', 'tp'))
Inputs may be any that keep to these rules, and one draw needn't show every extreme that they name: `queries`: query entries lie in -6 to 6. `cache`: cache entries lie in -6 to 6. `lengths`: each instance has a slot of length 1024. `prefix_blocks`: in each row the valid ids come first, then -1; more than half of a row's 16 entries are valid. Over the 8 rows of one instance, every owner (id // 8) is named at least once and at most 2 times, and some owner exactly 2 times.
All inputs are finite; a program needn't handle non-finite values.
Results may differ from a plain program's by a relative error of at most 0.013.
Values may be sent and summed in bfloat16 or wider, within the bound.
No kernel may reach another device: no remote copies, remote signals or barrier semaphores. Data moves between devices by JAX's collectives and lax.ppermute only.
A program may use at most 64 MiB of HBM per device.

v0:
```python
import jax
import jax.numpy as jnp
from jax import lax
from jax.sharding import PartitionSpec as P

QH = 64
KVH = 8
HD = 128
BLK = 128
CAP = 2


MASK_VALUE = -1e30


def partner(x, axis, stride):
    return lax.ppermute(x, axis, [(i, i ^ 1 << stride) for i in range(lax.axis_size(axis))])


def block_partials(query_rows, blocks, valid_mask):
    head_width = query_rows.shape[-1]
    key_part = blocks[..., :head_width]
    value_part = blocks[..., head_width:]
    scores = jnp.einsum(
        "nhgd,nbthd->nbhgt", query_rows, key_part, preferred_element_type=jnp.float32
    ) * head_width ** (-0.5)
    keep_mask = valid_mask[:, :, None, None, :]
    peak_score = jnp.max(jnp.where(keep_mask, scores, MASK_VALUE), axis=-1)
    weights = jnp.where(keep_mask, jnp.exp(scores - peak_score[..., None]), 0.0)
    weight_sum = jnp.sum(weights, axis=-1)
    blended = jnp.einsum(
        "nbhgt,nbthd->nbhgd",
        weights.astype(jnp.bfloat16),
        value_part,
        preferred_element_type=jnp.float32,
    )
    return (peak_score, weight_sum, blended)


def on_device(queries, new_kv, cache, lengths, migrate_slot, pool, prefix_blocks):
    row_count = queries.shape[0]
    head_count = new_kv.shape[1] // (2 * HD)
    group_count = QH // KVH
    inst_count = lax.axis_size("inst")
    partner_bit = inst_count.bit_length() - 2
    capacity = CAP
    span_count = cache.shape[1] // BLK
    query_heads = queries.reshape(row_count, head_count, group_count, HD)
    resident = cache.reshape(row_count, span_count, BLK, head_count, 2 * HD)
    stamps = jnp.arange(cache.shape[1], dtype=jnp.int32).reshape(span_count, BLK)
    mig_slot = migrate_slot[0]
    moving = jnp.arange(row_count, dtype=jnp.int32) == mig_slot
    pick_small = moving[:, None, None, None]
    pick_large = moving[:, None, None, None, None]
    moving_rows, moving_length = partner(
        (
            lax.dynamic_slice_in_dim(cache, mig_slot, 1, 0),
            lax.dynamic_slice_in_dim(lengths, mig_slot, 1, 0),
        ),
        "inst",
        partner_bit,
    )
    res_peak, res_sum, res_blend = block_partials(
        query_heads, resident, stamps[None] < lengths[:, None, None]
    )
    own_query = lax.dynamic_slice_in_dim(query_heads, mig_slot, 1, 0)
    moved_blocks = moving_rows.reshape(1, span_count, BLK, head_count, 2 * HD)
    mov_peak, mov_sum, mov_blend = block_partials(
        own_query, moved_blocks, stamps[None] < moving_length[:, None, None]
    )
    res_peak = jnp.where(pick_small, mov_peak, res_peak)
    res_sum = jnp.where(pick_small, mov_sum, res_sum)
    res_blend = jnp.where(pick_large, mov_blend, res_blend)
    entry_ids = prefix_blocks.reshape(-1)
    entry_count = entry_ids.shape[0]
    slots_per_row = prefix_blocks.shape[1]
    pool_count = pool.shape[0]
    has_block = entry_ids >= 0
    owner_id = jnp.where(has_block, entry_ids // pool_count, -1)
    local_id = jnp.where(has_block, entry_ids % pool_count, 0)
    owner_hit = owner_id[:, None] == jnp.arange(inst_count, dtype=jnp.int32)[None, :]
    owner_rank = jnp.sum(
        jnp.where(owner_hit, jnp.cumsum(owner_hit.astype(jnp.int32), axis=0) - 1, 0), axis=1
    )
    target_slot = jnp.where(has_block, owner_id * capacity + owner_rank, -1)
    slot_count = inst_count * capacity
    slot_hit = target_slot[:, None] == jnp.arange(slot_count, dtype=jnp.int32)[None, :]
    asked_ids = jnp.sum(jnp.where(slot_hit, local_id[:, None] + 1, 0), axis=0) - 1
    entry_request = jnp.arange(entry_count, dtype=jnp.int32) // slots_per_row
    slot_request = jnp.sum(jnp.where(slot_hit, entry_request[:, None], 0), axis=0)
    slot_used = jnp.any(slot_hit, axis=0)
    slot_query = jnp.take(query_heads, slot_request, axis=0)
    owner_asked = lax.all_to_all(
        asked_ids.reshape(inst_count, capacity), "inst", split_axis=0, concat_axis=0, tiled=True
    )
    fetched = jnp.take(pool, jnp.maximum(owner_asked.reshape(-1), 0), axis=0)
    arrived_blocks = lax.all_to_all(
        fetched.reshape(inst_count, capacity, BLK, -1),
        "inst",
        split_axis=0,
        concat_axis=0,
        tiled=True,
    )
    used_mask = jnp.broadcast_to(slot_used[:, None, None], (slot_count, 1, BLK))
    pre_peak, pre_sum, pre_blend = block_partials(
        slot_query, arrived_blocks.reshape(slot_count, 1, BLK, head_count, 2 * HD), used_mask
    )
    fresh_mask = jnp.zeros((row_count, 1, 1), jnp.int32) == 0
    new_peak, new_sum, new_blend = block_partials(
        query_heads, new_kv.reshape(row_count, 1, 1, head_count, 2 * HD), fresh_mask
    )
    slot_peak = pre_peak[:, 0]
    slot_sum = pre_sum[:, 0]
    slot_blend = pre_blend[:, 0]
    member = (slot_request[:, None] == jnp.arange(row_count, dtype=jnp.int32)[None, :]) & slot_used[
        :, None
    ]
    prefix_best = jnp.max(
        jnp.where(member[:, :, None, None], slot_peak[:, None], MASK_VALUE), axis=0
    )
    top_score = jnp.maximum(jnp.maximum(jnp.max(res_peak, axis=1), prefix_best), new_peak[:, 0])
    res_scale = jnp.exp(res_peak - top_score[:, None])
    numerator = jnp.sum(res_scale[..., None] * res_blend, axis=1)
    denominator = jnp.sum(res_scale * res_sum, axis=1)
    slot_scale = jnp.where(
        slot_used[:, None, None],
        jnp.exp(slot_peak - jnp.take(top_score, slot_request, axis=0)),
        0.0,
    )
    member_float = member.astype(jnp.float32)
    numerator = numerator + jnp.einsum(
        "sr,shgd->rhgd",
        member_float,
        slot_scale[..., None] * slot_blend,
        precision=lax.Precision.HIGHEST,
    )
    denominator = denominator + jnp.einsum(
        "sr,shg->rhg", member_float, slot_scale * slot_sum, precision=lax.Precision.HIGHEST
    )
    new_scale = jnp.exp(new_peak[:, 0] - top_score)
    numerator = numerator + new_scale[..., None] * new_blend[:, 0]
    denominator = denominator + new_scale * new_sum[:, 0]
    attended = (numerator / denominator[..., None]).astype(jnp.bfloat16).reshape(row_count, -1)
    return lax.all_to_all(attended, "tp", split_axis=0, concat_axis=1, tiled=True)


def solution(mesh):
    in_specs = (
        P("inst", "tp"),
        P("inst", "tp"),
        P("inst", None, "tp"),
        P("inst"),
        P("inst"),
        P("inst", None, "tp"),
        P("inst", None),
    )
    out_specs = P(("inst", "tp"), None)
    return jax.shard_map(
        on_device, mesh=mesh, in_specs=in_specs, out_specs=out_specs, check_vma=False
    )
```

profile of v0, /device:TPU:1, one launch (start us, length us, event | category | flops | bytes accessed | tf_op | source)
XLA Modules:
  0.0 269.4 jit_solution(16211051527744112539)
XLA Ops:
  0.0 0.8 reshape.549
  0.8 0.1 fusion.33
  0.9 0.2 reduce_window_sum.11
  1.1 0.2 select_reduce_fusion.4
  1.3 0.1 select_reduce_fusion.3
  1.4 0.1 sub.91
  1.6 24.4 %all_to_all.27 = s32[64,1,2]{2,1,0:T(1,128)S(1)} all-to-all(s32[64,1,2]{2,1,0:T(1,128)S(1)} %bitcast.138), channel_id=1, replica_groups=mesh['inst'=64,'tp'=8] {'inst'}, dimensions={0} | all-to-all | bytes 1024 | tf_op jit(solution)/shard_map/all_to_all | solution.py:93
  26.0 0.1 maximum_reduce_fusion
  26.1 0.1 reshape.564
  26.3 0.1 copy.74
  26.4 0.1 copy.75
  26.6 6.5 %gather_fusion = bf16[128,128,256]{2,1,0:T(8,128)(2,1)} fusion(bf16[8,128,256]{2,1,0:T(8,128)(2,1)S(1)} %copy-done, s32[1024]{0:T(1024)S(1)} %pad_clamp_fusion.1), kind=kCustom, calls=%fused_computation | custom fusion | bytes 16777728 | tf_op jit(solution)/shard_map/jit(_take)/gather | solution.py:96
  33.1 7.4 %broadcast_select_fusion = bf16[64,2,128,256]{3,2,1,0:T(8,128)(2,1)} fusion(bf16[64,2,128,256]{3,2,1,0:T(8,128)(2,1)} %bitcast.133, pred[64,2]{1,0:T(8,128)(4,1)S(1)} %copy.75), kind=kLoop, calls=%fused_computation.3 | loop fusion | flops 4194304 | bytes 16777344 | tf_op jit(solution)/shard_map/jit(_take)/select_n | solution.py:96
  40.5 5.9 %all-to-all-start.1 = ((bf16[64,2,128,256]{3,2,1,0:T(8,128)(2,1)}), bf16[64,2,128,256]{3,2,1,0:T(8,128)(2,1)}, u32[]{:S(2)}, u32[]{:S(2)}) async-start(bf16[64,2,128,256]{3,2,1,0:T(8,128)(2,1)} %broadcast_select_fusion), calls=%async_computation.1 | async-start | bytes 16777216 | tf_op jit(solution)/shard_map/all_to_all | solution.py:97
  47.1 0.6 dynamic_slice.9
  47.7 2.9 %collective-permute-start = (s32[1]{0:T(128)}, s32[1]{0:T(128)}, u32[]{:S(2)}, u32[]{:S(2)}) collective-permute-start(s32[1]{0:T(128)} %dynamic_slice.9), channel_id=1, source_target_pairs={{0,256},{8,264},{16,272},{24,280},{32,288},{40,296},{48,304},{56,3... | collective-permute-start | bytes 20 | tf_op jit(solution)/shard_map/ppermute | solution.py:17
  50.6 1.1 constant_dynamic-slice_fusion.1
  51.7 2.3 collective-permute-start.1
  54.1 0.7 gather_fusion.1
  54.8 0.1 fusion.32
  54.9 0.1 broadcast_compare_fusion
  55.0 2.3 select_reduce_fusion.1
  57.3 0.3 bitcast_reduce_fusion.1
  57.7 0.1 fusion.41
  57.8 113.3 %collective-permute-done = s32[1]{0:T(128)} collective-permute-done((s32[1]{0:T(128)}, s32[1]{0:T(128)}, u32[]{:S(2)}, u32[]{:S(2)}) %collective-permute-start) | collective-permute-done | bytes 36 | tf_op jit(solution)/shard_map/ppermute | solution.py:17
  171.0 0.7 broadcast_compare_fusion.1
  171.7 11.1 %collective-permute-done.1 = bf16[1,1024,256]{2,1,0:T(8,128)(2,1)S(1)} collective-permute-done((bf16[1,1024,256]{2,1,0:T(8,128)(2,1)S(1)}, bf16[1,1024,256]{2,1,0:T(8,128)(2,1)S(1)}, u32[]{:S(2)}, u32[]{:S(2)}) %collective-permute-start.1) | collective-permute-done | bytes 524320 | tf_op jit(solution)/shard_map/ppermute | solution.py:17
  182.8 0.2 select_reduce_fusion.6
  183.1 0.1 select_reduce_fusion.7
  183.2 0.2 bitcast_reduce_fusion.2
  183.4 0.2 fusion.18
  183.6 54.7 %all-to-all-done.1 = bf16[64,2,128,256]{3,2,1,0:T(8,128)(2,1)} async-done(((bf16[64,2,128,256]{3,2,1,0:T(8,128)(2,1)}), bf16[64,2,128,256]{3,2,1,0:T(8,128)(2,1)}, u32[]{:S(2)}, u32[]{:S(2)}) %all-to-all-start.1) | async-done | bytes 8388640 | tf_op jit(solution)/shard_map/all_to_all | solution.py:97
  238.3 4.4 %select_reduce_fusion = (f32[128,8]{1,0:T(8,128)S(1)}, f32[128,1,1,128,8]{3,4,0,2,1:T(8,128)S(1)}) fusion(pred[128]{0:T(512)(128)(4,1)S(1)} %fusion.32, bf16[128,8,128]{2,1,0:T(8,128)(2,1)S(1)} %gather_fusion.1, pred[128]{0:T(512)(128)(4,1)S(1)} %compare_and_fusion, bf16[128,1,128,1,256]{4,2,0,3,1:T(8,128)(2,1)} %bitcast.15), kind=kOutput, calls=%fused_computation.30 | convolution fusion | flops 34077696 | bytes 4985088 | tf_op jit(solution)/shard_map/nhgd,nbthd->nbhgt/dot_general | solution.py:24
  242.7 0.5 bitcast_reduce_fusion
  243.3 0.1 select_reduce_fusion.5
  243.4 0.6 gather_fusion.2
  244.1 0.1 copy.79
  244.3 0.1 multiply_reduce_fusion.1
  244.4 0.1 fusion.14
  244.5 0.1 copy.85
  244.6 3.1 %fusion.4 = f32[128,8,128]{2,1,0:T(8,128)S(1)} fusion(bf16[128,1,128,1,256]{4,2,0,3,1:T(8,128)(2,1)} %bitcast.15, f32[128,1,1,128,8]{3,4,0,2,1:T(8,128)S(1)} %get-tuple-element.17, f32[128,8]{1,0:T(8,128)S(1)} %get-tuple-element.16, f32[128,8]{1,0:T(8,128)S(1)} %copy.79, pred[128]{0:T(512)(128)(4,1)S(1)} %fusion.32), kind=kOutput, calls=%fused_computation.12 | convolution fusion | flops 34078720 | bytes 5251200 | tf_op jit(solution)/shard_map/nbhgt,nbthd->nbhgd/dot_general | solution.py:31
  247.6 0.1 copy.82
  247.8 2.3 multiply_reduce_fusion
  250.1 0.3 fusion.13
  250.5 0.5 broadcast.520
  251.0 0.7 reduce.20
  251.7 17.1 %all_to_all.28 = bf16[8,2,512]{2,1,0:T(2,128)(2,1)S(1)} all-to-all(bf16[8,2,512]{2,1,0:T(2,128)(2,1)S(1)} %reshape.608), channel_id=1, replica_groups=mesh['inst'=64,'tp'=8] {'tp'}, dimensions={0} | all-to-all | bytes 32768 | tf_op jit(solution)/shard_map/all_to_all | solution.py:144
  268.8 0.6 reshape.609
  (29 shorter events, 0.4 us)
Async XLA Ops:
  0.0 26.6 %copy-start = (bf16[8,128,256]{2,1,0:T(8,128)(2,1)S(1)}, bf16[8,128,256]{2,1,0:T(8,128)(2,1)}, u32[]{:S(2)}) copy-start(bf16[8,128,256]{2,1,0:T(8,128)(2,1)} %param.12) | copy-start | bytes 1572868
  40.5 6.6 %copy-start.3 = (s32[8]{0:T(128)S(1)}, s32[8]{0:T(128)}, u32[]{:S(2)}) copy-start(s32[8]{0:T(128)} %param.10) | copy-start | bytes 100
  40.5 13.6 %copy-start.1 = (bf16[8,1024]{1,0:T(8,128)(2,1)S(1)}, bf16[8,1024]{1,0:T(8,128)(2,1)}, u32[]{:S(2)}) copy-start(bf16[8,1024]{1,0:T(8,128)(2,1)} %param.7) | copy-start | bytes 49156
  40.5 197.8 %all-to-all-start.1 = ((bf16[64,2,128,256]{3,2,1,0:T(8,128)(2,1)}), bf16[64,2,128,256]{3,2,1,0:T(8,128)(2,1)}, u32[]{:S(2)}, u32[]{:S(2)}) async-start(bf16[64,2,128,256]{3,2,1,0:T(8,128)(2,1)} %broadcast_select_fusion), calls=%async_computation.1 | async-start | bytes 16777216 | tf_op jit(solution)/shard_map/all_to_all | solution.py:97
  46.4 11.2 %copy-start.2 = (bf16[8,256]{1,0:T(8,128)(2,1)S(1)}, bf16[8,256]{1,0:T(8,128)(2,1)}, u32[]{:S(2)}) copy-start(bf16[8,256]{1,0:T(8,128)(2,1)} %param.8) | copy-start | bytes 12292
  47.7 123.4 %collective-permute-start = (s32[1]{0:T(128)}, s32[1]{0:T(128)}, u32[]{:S(2)}, u32[]{:S(2)}) collective-permute-start(s32[1]{0:T(128)} %dynamic_slice.9), channel_id=1, source_target_pairs={{0,256},{8,264},{16,272},{24,280},{32,288},{40,296},{48,304},{56,3... | collective-permute-start | bytes 20 | tf_op jit(solution)/shard_map/ppermute | solution.py:17
  51.7 131.1 %collective-permute-start.1 = (bf16[1,1024,256]{2,1,0:T(8,128)(2,1)S(1)}, bf16[1,1024,256]{2,1,0:T(8,128)(2,1)S(1)}, u32[]{:S(2)}, u32[]{:S(2)}) collective-permute-start(bf16[1,1024,256]{2,1,0:T(8,128)(2,1)S(1)} %constant_dynamic-slice_fusion.1), channel_id=1, source_target_pairs={{0,256},{8,264},{16,272},{24,280},{32,288},{40,296},{48,304},{56,3... | collective-permute-start | bytes 1572872 | tf_op jit(solution)/shard_map/ppermute | solution.py:17
where the time goes:
time: 270 us; the launch traced here: 269 us
  waiting for transfers between devices  179 us (66%)
  blocking collectives  41.6 us (15%)
  matrix products  13.2 us (5%)
  local copies, waits for them, and re-layouts  12.5 us (5%)
  starting transfers between devices  11.2 us (4%)
  other arithmetic  11 us (4%)
    ppermute x2, waiting for transfers between devices, partner(): lax.ppermute(x, axis, [(i, i ^ 1 << stride) for i in range(lax.axis_size(...  124 us
    all_to_all x1, waiting for transfers between devices, on_device(): lax.all_to_all(fetched.reshape(inst_count, capacity, BLK, -1), 'inst', sp...  54.7 us
    all_to_all x1, blocking collectives, on_device(): lax.all_to_all(asked_ids.reshape(inst_count, capacity), 'inst', split_axi...  24.4 us
    all_to_all x1, blocking collectives, on_device(): lax.all_to_all(attended, 'tp', split_axis=0, concat_axis=1, tiled=True)  17.1 us
    select_n x1, other arithmetic, on_device(): fetched = jnp.take(pool, jnp.maximum(owner_asked.reshape(-1), 0), axis=0)  7.42 us
    dot_general x4, matrix products, block_partials(): jnp.einsum('nhgd,nbthd->nbhgt', query_rows, key_part, preferred_element_t...  7.11 us
    gather x1, local copies, waits for them, and re-layouts, on_device(): fetched = jnp.take(pool, jnp.maximum(owner_asked.reshape(-1), 0), axis=0)  6.51 us
    all_to_all x1, starting transfers between devices, on_device(): lax.all_to_all(fetched.reshape(inst_count, capacity, BLK, -1), 'inst', sp...  5.89 us
  transfers between devices with their start and end apart: 3, of which 3 were waited for; matrix products, arithmetic and copies ran while one was open for 3% of the time, Pallas kernels for 0%

commit v1 on v0

v1 whole, which is shorter than its diff:
```python
import jax
import jax.numpy as jnp
from jax import lax
from jax.experimental import pallas as pl
from jax.experimental.pallas import tpu as pltpu
from jax.sharding import PartitionSpec as P

QH = 64
KVH = 8
HD = 128
BLK = 128
GRP = QH // KVH
CAP = 2
NONE = 8191
FIRST = 20
FIRST_TP = 4
TAIL = 16
HEADS = 2
TOGETHER = 4
ROWS = 18
SCALE = HD**-0.5
LOW = -1e30
MIB = 1024 * 1024

NT = (((1,), (1,)), ((), ()))
NN = (((1,), (0,)), ((), ()))


def dot(a, b, dims):
    return lax.dot_general(a, b, dims, preferred_element_type=jnp.float32)


def in_hbm(x):
    return pltpu.with_memory_space_constraint(x, pltpu.HBM)


def lanes(shape):
    return lax.broadcasted_iota(jnp.int32, shape, len(shape) - 1)


def slot_codes(ids, insts):
    rows, width = ids.shape
    slots = CAP * insts
    lane = (lanes((rows, slots)) & (insts - 1)) ^ FIRST
    row = lax.broadcasted_iota(jnp.int32, (rows, slots), 0)
    first = jnp.full((rows, slots), NONE, jnp.int32)
    last = jnp.full((rows, slots), -1, jnp.int32)
    for e in range(width):
        entry = jnp.broadcast_to(ids[:, e : e + 1], (rows, slots))
        named = (entry >= 0) & ((entry >> 3) == lane)
        code = (row * width + e) * 8 + (entry & 7)
        first = jnp.where(named, jnp.minimum(first, code), first)
        last = jnp.where(named, code, last)
    first = jnp.min(first.astype(jnp.float32), axis=0, keepdims=True)
    last = jnp.max(last.astype(jnp.float32), axis=0, keepdims=True)
    second = jnp.where(last > first, last, float(NONE))
    return jnp.where(lanes((1, slots)) < insts, first, second)


def pack_kernel(prefix_hbm, queries_hbm, out, heads, stage, flat, prefix, queries, sems):
    fetch_prefix = pltpu.make_async_copy(prefix_hbm, prefix, sems.at[0])
    fetch_queries = pltpu.make_async_copy(queries_hbm, queries, sems.at[1])
    fetch_prefix.start()
    fetch_queries.start()
    insts = stage.shape[0] // ROWS
    for r in range(CAP * GRP + 1, ROWS):
        stage[pl.ds(r, insts, stride=ROWS), :] = jnp.zeros((insts, HD), jnp.float32)
    fetch_prefix.wait()
    slots = CAP * insts
    codes = jnp.broadcast_to(slot_codes(prefix[...], insts), (slots, slots)).T.astype(jnp.int32)
    pick = ((codes >> 7) == lanes(codes.shape))[:, :GRP].astype(jnp.float32).astype(jnp.bfloat16)
    fetch_queries.wait()
    picked = dot(pick, queries[...], NN)
    lane = lanes((insts, HD))
    local = (codes & 7).astype(jnp.float32)
    ids = jnp.where(lane == 0, local[:insts], jnp.where(lane == 1, local[insts:], 0.0))
    for k in range(CAP):
        for g in range(GRP):
            part = picked[k * insts : (k + 1) * insts, g * HD : (g + 1) * HD]
            stage[pl.ds(k * GRP + g, insts, stride=ROWS), :] = part
    stage[pl.ds(CAP * GRP, insts, stride=ROWS), :] = ids
    out[...] = stage[...].astype(jnp.bfloat16)
    own = queries[...].astype(jnp.float32)
    for g in range(GRP):
        flat[pl.ds(g, own.shape[0], stride=GRP), :] = own[:, g * HD : (g + 1) * HD]
    heads[...] = flat[...].astype(jnp.bfloat16)


def pack(insts, prefix, queries):
    size = insts * ROWS
    flat = queries.shape[0] * GRP
    hbm = pl.BlockSpec(memory_space=pltpu.HBM)
    vmem = pl.BlockSpec(memory_space=pltpu.VMEM)
    return pl.pallas_call(
        pack_kernel,
        out_shape=[
            jax.ShapeDtypeStruct((size, HD), jnp.bfloat16),
            jax.ShapeDtypeStruct((flat, HD), jnp.bfloat16),
        ],
        in_specs=[hbm, hbm],
        out_specs=[vmem, vmem],
        scratch_shapes=[
            pltpu.VMEM((size, HD), jnp.float32),
            pltpu.VMEM((flat, HD), jnp.float32),
            pltpu.VMEM(prefix.shape, prefix.dtype),
            pltpu.VMEM(queries.shape, queries.dtype),
            pltpu.SemaphoreType.DMA((2,)),
        ],
        compiler_params=pltpu.CompilerParams(vmem_limit_bytes=8 * MIB),
        cost_estimate=pl.CostEstimate(flops=1 << 22, bytes_accessed=1 << 19, transcendentals=0),
        name="pack",
    )(in_hbm(prefix), in_hbm(queries))


def attend(queries, cache, slots, lengths):
    scores = [dot(q, cache[s, :, :HD], NT) * SCALE for q, s in zip(queries, slots)]
    valid = [lanes(x.shape) < jnp.broadcast_to(n, x.shape) for x, n in zip(scores, lengths)]
    peaks = [
        jnp.max(jnp.where(v, x, LOW), axis=1, keepdims=True) for x, v in zip(scores, valid)
    ]
    weights = [jnp.where(v, jnp.exp(x - p), 0.0) for x, v, p in zip(scores, valid, peaks)]
    mixes = [dot(w.astype(jnp.bfloat16), cache[s, :, HD:], NN) for w, s in zip(weights, slots)]
    totals = [jnp.sum(w, axis=1, keepdims=True) for w in weights]
    stats = [jnp.where(lanes((GRP, HD)) == 0, p, t) for p, t in zip(peaks, totals)]
    return mixes, stats


def prepare_kernel(mig, lengths, pool_hbm, cache_hbm, keys, values, leaving, pool, sems):
    tokens = cache_hbm.shape[1]
    fetch_pool = pltpu.make_async_copy(pool_hbm, pool, sems.at[0])
    fetch_row = pltpu.make_async_copy(
        cache_hbm.at[mig[0]], leaving.at[pl.ds(0, tokens)], sems.at[1]
    )
    fetch_pool.start()
    fetch_row.start()
    length = lengths[mig[0]]
    lane = lanes((TAIL, leaving.shape[1]))
    tail = jnp.where(lane == 0, length >> 3, jnp.where(lane == 1, length & 7, 0))
    leaving[tokens:] = tail.astype(jnp.float32).astype(jnp.bfloat16)
    fetch_pool.wait()
    half = pool.shape[0] // BLK // 2
    for p in range(half):
        for b in range(2):
            block = slice((2 * p + b) * BLK, (2 * p + b + 1) * BLK)
            keys[p * BLK : (p + 1) * BLK, b * HD : (b + 1) * HD] = pool[block, :HD]
    for b in range(2):
        part = slice(b * half * BLK, (b + 1) * half * BLK)
        values[:, b * HD : (b + 1) * HD] = pool[part, HD:]
    fetch_row.wait()


def prepare(mig, lengths, pool, cache):
    rows, tokens, width = cache.shape
    smem = pl.BlockSpec(memory_space=pltpu.SMEM)
    vmem = pl.BlockSpec(memory_space=pltpu.VMEM)
    hbm = pl.BlockSpec(memory_space=pltpu.HBM)
    paired = jax.ShapeDtypeStruct((pool.shape[0] // 2, 2 * HD), pool.dtype)
    return pl.pallas_call(
        prepare_kernel,
        out_shape=[paired, paired, jax.ShapeDtypeStruct((tokens + TAIL, width), cache.dtype)],
        in_specs=[smem, smem, hbm, hbm],
        out_specs=[vmem, vmem, vmem],
        scratch_shapes=[pltpu.VMEM(pool.shape, pool.dtype), pltpu.SemaphoreType.DMA((2,))],
        compiler_params=pltpu.CompilerParams(vmem_limit_bytes=8 * MIB),
        cost_estimate=pl.CostEstimate(
            flops=0, bytes_accessed=2 * (pool.size + tokens * width), transcendentals=0
        ),
        name="prepare",
    )(mig, lengths, in_hbm(pool), in_hbm(cache))


def resident_kernel(
    mig, lengths, query, new_kv_hbm, moved, cache_hbm, out, cache, tail, new_kv, sems, sem_tail, sem_new
):
    rows, tokens, _ = cache.shape
    fetch_tail = pltpu.make_async_copy(moved.at[pl.ds(tokens, TAIL)], tail, sem_tail)
    fetch_new = pltpu.make_async_copy(new_kv_hbm, new_kv, sem_new)
    fetch_tail.start()
    fetch_new.start()
    fetches = []
    for s in range(rows):
        here = pltpu.make_async_copy(cache_hbm.at[s], cache.at[s], sems.at[s])
        came = pltpu.make_async_copy(moved.at[pl.ds(0, tokens)], cache.at[s], sems.at[s])
        pl.when(mig[0] != s)(here.start)
        pl.when(mig[0] == s)(came.start)
        fetches.append(here)
    fetch_tail.wait()
    fetch_new.wait()
    parts = tail[...].astype(jnp.float32)
    moved_length = (parts[0:1, 0:1] * 8.0 + parts[0:1, 1:2]).astype(jnp.int32)
    length = [jnp.where(mig[0] == s, moved_length, lengths[s]) for s in range(rows)]
    key = new_kv[:, :HD].astype(jnp.float32)
    fresh = [
        jnp.sum(query[s].astype(jnp.float32) * key[s : s + 1], axis=1, keepdims=True) * SCALE
        for s in range(rows)
    ]
    for c in range(0, rows, TOGETHER):
        slots = range(c, c + TOGETHER)
        for s in slots:
            fetches[s].wait()
        mixes, stats = attend([query[s] for s in slots], cache, slots, [length[s] for s in slots])
        for s, mix, stat in zip(slots, mixes, stats):
            out[s, :GRP] = mix
            out[s, GRP:] = jnp.where(lanes((GRP, HD)) == 2, fresh[s], stat)


def resident(mig, lengths, query, new_kv, moved, cache):
    rows, tokens, width = cache.shape
    smem = pl.BlockSpec(memory_space=pltpu.SMEM)
    vmem = pl.BlockSpec(memory_space=pltpu.VMEM)
    hbm = pl.BlockSpec(memory_space=pltpu.HBM)
    return pl.pallas_call(
        resident_kernel,
        out_shape=jax.ShapeDtypeStruct((rows, 2 * GRP, HD), jnp.float32),
        in_specs=[smem, smem, vmem, hbm, pl.BlockSpec(memory_space=pl.ANY), hbm],
        out_specs=vmem,
        scratch_shapes=[
            pltpu.VMEM(cache.shape, cache.dtype),
            pltpu.VMEM((TAIL, width), cache.dtype),
            pltpu.VMEM(new_kv.shape, new_kv.dtype),
            pltpu.SemaphoreType.DMA((rows,)),
            pltpu.SemaphoreType.DMA,
            pltpu.SemaphoreType.DMA,
        ],
        compiler_params=pltpu.CompilerParams(vmem_limit_bytes=12 * MIB),
        cost_estimate=pl.CostEstimate(
            flops=1 << 34, bytes_accessed=1 << 26, transcendentals=rows * GRP * tokens
        ),
        name="resident",
    )(mig, lengths, query, in_hbm(new_kv), moved, in_hbm(cache))


def owner_kernel(arrived, keys, values, out, stage):
    stage[...] = arrived[...].astype(jnp.float32)
    insts = stage.shape[0] // ROWS
    slots = CAP * insts
    half = keys.shape[0] // BLK

    def rows_of(r):
        return stage[pl.ds(r, insts, stride=ROWS), :]

    ids = rows_of(CAP * GRP)
    local = jnp.concatenate([ids[:, k : k + 1] for k in range(CAP)], axis=0).astype(jnp.int32)
    local = jnp.broadcast_to(local, (slots, BLK))
    odd = (local & 1) == 1
    pair = jnp.concatenate([local >> 1] * HEADS, axis=0)
    rest = jnp.concatenate([local & (half - 1)] * HEADS, axis=0)
    upper = jnp.concatenate([local >= half] * HEADS, axis=0)
    lane = lanes((slots, HD))

    def score(c):
        query = []
        for g in range(c * HEADS, (c + 1) * HEADS):
            part = jnp.concatenate([rows_of(k * GRP + g) for k in range(CAP)], axis=0)
            halves = [jnp.where(odd, 0.0, part), jnp.where(odd, part, 0.0)]
            query.append(jnp.concatenate(halves, axis=1).astype(jnp.bfloat16))
        return dot(jnp.concatenate(query, axis=0), keys[...], NT)

    def weigh(scores):
        picked = scores[:, :BLK]
        for p in range(1, half):
            picked = jnp.where(pair == p, scores[:, p * BLK : (p + 1) * BLK], picked)
        picked = picked * SCALE
        peak = jnp.max(picked, axis=1, keepdims=True).astype(jnp.bfloat16).astype(jnp.float32)
        weights = jnp.exp(picked - peak)
        total = jnp.sum(weights, axis=1, keepdims=True)
        spread = [jnp.where(rest == b, weights, 0.0).astype(jnp.bfloat16) for b in range(half)]
        return jnp.concatenate(spread, axis=1), peak, total

    def mix(spread):
        both = dot(spread, values[...], NN)
        return jnp.where(upper, both[:, HD:], both[:, :HD])

    chunks = GRP // HEADS
    stats = jnp.zeros((slots, HD), jnp.float32)
    mixes = []
    scores = score(0)
    waiting = None
    for c in range(chunks):
        following = score(c + 1) if c + 1 < chunks else None
        spread, peak, total = weigh(scores)
        if waiting is not None:
            mixes.append(mix(waiting))
        total_hi = total.astype(jnp.bfloat16).astype(jnp.float32)
        total_lo = total - total_hi
        for h in range(HEADS):
            g = c * HEADS + h
            part = slice(h * slots, (h + 1) * slots)
            stats = jnp.where(lane == g, peak[part], stats)
            stats = jnp.where(lane == GRP + g, total_hi[part], stats)
            stats = jnp.where(lane == 2 * GRP + g, total_lo[part], stats)
        scores, waiting = following, spread
    mixes.append(mix(waiting))
    for k in range(CAP):
        for g in range(GRP):
            start = g % HEADS * slots + k * insts
            part = mixes[g // HEADS][start : start + insts]
            stage[pl.ds(k * GRP + g, insts, stride=ROWS), :] = part
        stage[pl.ds(CAP * GRP + k, insts, stride=ROWS), :] = stats[k * insts : (k + 1) * insts]
    out[...] = stage[...].astype(jnp.bfloat16)


def owner(arrived, keys, values):
    vmem = pl.BlockSpec(memory_space=pltpu.VMEM)
    return pl.pallas_call(
        owner_kernel,
        out_shape=jax.ShapeDtypeStruct(arrived.shape, jnp.bfloat16),
        in_specs=[vmem, vmem, vmem],
        out_specs=vmem,
        scratch_shapes=[pltpu.VMEM(arrived.shape, jnp.float32)],
        compiler_params=pltpu.CompilerParams(vmem_limit_bytes=24 * MIB),
        cost_estimate=pl.CostEstimate(
            flops=1 << 29, bytes_accessed=2 << 20, transcendentals=1 << 17
        ),
        name="owner",
    )(arrived, keys, values)


def combine_kernel(prefix, arrived, own, new_kv, out, wide, table):
    wide[...] = arrived[...].astype(jnp.float32)
    insts = wide.shape[0] // ROWS
    rows = own.shape[0]
    slots = CAP * insts
    codes = slot_codes(prefix[...], insts).astype(jnp.int32)
    belongs = jnp.where(codes < NONE, codes >> 7, -1)

    def rows_of(r):
        return wide[pl.ds(r, insts, stride=ROWS), :]

    stats = jnp.concatenate([rows_of(CAP * GRP + k) for k in range(CAP)], axis=0).T
    peak = stats[:GRP]
    total = stats[GRP : 2 * GRP] + stats[2 * GRP : 3 * GRP]
    values = new_kv[:, HD:].astype(jnp.float32)
    below, mixes = [], []
    for s in range(rows):
        mine = jnp.broadcast_to(belongs, (GRP, slots)) == s
        stat = own[s, GRP:]
        res_peak, res_total, new_peak = stat[:, 0:1], stat[:, 1:2], stat[:, 2:3]
        top = jnp.max(jnp.where(mine, peak, LOW), axis=1, keepdims=True)
        top = jnp.maximum(jnp.maximum(top, res_peak), new_peak)
        weight = jnp.where(mine, jnp.exp(jnp.where(mine, peak, LOW) - top), 0.0)
        table[s * GRP : (s + 1) * GRP, :] = weight
        res_scale = jnp.exp(res_peak - top)
        new_scale = jnp.exp(new_peak - top)
        below.append(
            jnp.sum(weight * total, axis=1, keepdims=True) + res_scale * res_total + new_scale
        )
        mixes.append(
            res_scale * own[s, :GRP] + new_scale * values[s : s + 1]
        )
    sums = []
    for g in range(GRP):
        weight = table[pl.ds(g, rows, stride=GRP), :]
        weight_hi = weight.astype(jnp.bfloat16).astype(jnp.float32)
        both = jnp.concatenate([weight_hi, weight - weight_hi], axis=0).astype(jnp.bfloat16)
        mix = jnp.concatenate([rows_of(k * GRP + g) for k in range(CAP)], axis=0)
        got = dot(both, mix.astype(jnp.bfloat16), NN)
        sums.append(got[:rows] + got[rows:])
    for g in range(GRP):
        table[pl.ds(g, rows, stride=GRP), :] = sums[g]
    attended = [
        (table[s * GRP : (s + 1) * GRP, :] + mixes[s]) / below[s]
        for s in (r ^ FIRST_TP for r in range(rows))
    ]
    out[...] = jnp.concatenate(attended, axis=0).astype(jnp.bfloat16)


def combine(prefix, arrived, own, new_kv):
    rows = own.shape[0]
    vmem = pl.BlockSpec(memory_space=pltpu.VMEM)
    return pl.pallas_call(
        combine_kernel,
        out_shape=jax.ShapeDtypeStruct((rows * GRP, HD), jnp.bfloat16),
        in_specs=[vmem] * 4,
        out_specs=vmem,
        scratch_shapes=[
            pltpu.VMEM(arrived.shape, jnp.float32),
            pltpu.VMEM((rows * GRP, HD), jnp.float32),
        ],
        compiler_params=pltpu.CompilerParams(vmem_limit_bytes=8 * MIB),
        cost_estimate=pl.CostEstimate(flops=1 << 24, bytes_accessed=1 << 20, transcendentals=8192),
        name="combine",
    )(prefix, arrived, own, new_kv)


def on_device(queries, new_kv, cache, lengths, migrate_slot, pool, prefix_blocks):
    rows = queries.shape[0]
    insts = lax.axis_size("inst")
    swap = [(i, i ^ (insts // 2)) for i in range(insts)]
    order = [[r ^ FIRST for r in range(insts)]]
    order_tp = [[r ^ FIRST_TP for r in range(rows)]]

    def exchange(messages):
        messages = messages.reshape(insts, ROWS // 2, 2, HD)
        arrived = lax.all_to_all(
            messages, "inst", split_axis=0, concat_axis=0, axis_index_groups=order, tiled=True
        )
        return arrived.reshape(-1, HD)

    messages, query = pack(insts, prefix_blocks, queries)
    asked = exchange(messages)
    keys, values, leaving = prepare(migrate_slot, lengths, pool.reshape(-1, 2 * HD), cache)
    moved = lax.ppermute(leaving, "inst", swap)
    answers = exchange(owner(asked, keys, values))
    query = query.reshape(rows, GRP, HD)
    own = resident(migrate_slot, lengths, query, new_kv, moved, cache)
    attended = combine(prefix_blocks, answers, own, new_kv)
    attended = attended.reshape(rows, GRP, HD)
    heads = lax.all_to_all(
        attended, "tp", split_axis=0, concat_axis=0, axis_index_groups=order_tp, tiled=True
    )
    heads = jnp.concatenate([heads[FIRST_TP:], heads[:FIRST_TP]], axis=0)
    return heads.reshape(1, -1)


def solution(mesh):
    in_specs = (
        P("inst", "tp"),
        P("inst", "tp"),
        P("inst", None, "tp"),
        P("inst"),
        P("inst"),
        P("inst", None, "tp"),
        P("inst", None),
    )
    out_specs = P(("inst", "tp"), None)
    return jax.shard_map(
        on_device, mesh=mesh, in_specs=in_specs, out_specs=out_specs, check_vma=False
    )
```

time: 270 us -> 59.2 us (0.22)
  waiting for transfers between devices: 179 us -> 4.33 us
  blocking collectives: 41.6 us -> 10.2 us
  starting transfers between devices: 11.2 us -> 33.1 us
  matrix products: 13.2 us -> 0 us
  local copies, waits for them, and re-layouts: 12.5 us -> 1.3 us
  other arithmetic: 11 us -> 0.01 us
  Pallas kernels: 0 us -> 9.13 us
    ppermute x2 -> x1, waiting for transfers between devices: 124 us -> 0.01 us  [on_device(): moved = lax.ppermute(leaving, 'inst', swap)]
    all_to_all x1 -> x2, waiting for transfers between devices: 54.7 us -> 4.33 us  [exchange(): lax.all_to_all(messages, 'inst', split_axis=0, concat_axis=0, axis_index_...]
    all_to_all x2 -> x1, blocking collectives: 41.6 us -> 10.2 us  [on_device(): lax.all_to_all(attended, 'tp', split_axis=0, concat_axis=0, axis_index_gr...]
    all_to_all x1 -> x2, starting transfers between devices: 5.89 us -> 29.8 us  [exchange(): lax.all_to_all(messages, 'inst', split_axis=0, concat_axis=0, axis_index_...]
    dot_general x9 -> x0, matrix products: 13.2 us -> none  [the longest x4 7.11 us: block_partials(): jnp.einsum('nhgd,nbthd->nbhgt', query_rows, key_part, preferred_element_t...]
    pallas_call x0 -> x5, Pallas kernels: none -> 9.13 us  [the longest x1 3.29 us: resident(): pl.pallas_call(resident_kernel, out_shape=jax.ShapeDtypeStruct((rows, 2 *...]
    gather x4 -> x0, local copies, waits for them, and re-layouts: 7.89 us -> none  [the longest x1 6.51 us: on_device(): fetched = jnp.take(pool, jnp.maximum(owner_asked.reshape(-1), 0), axis=0)]
    select_n x4 -> x0, other arithmetic: 7.44 us -> none  [the longest x1 7.42 us: on_device(): fetched = jnp.take(pool, jnp.maximum(owner_asked.reshape(-1), 0), axis=0)]
  transfers between devices with their start and end apart: 3 -> 3, of which waited for: 3 -> 2; matrix products, arithmetic and copies ran while one was open for 3% -> 0% of each run, Pallas kernels for 0% -> 12%
where the time goes in v1:
time: 59.2 us; the launch traced here: 58.8 us
  starting transfers between devices  33.1 us (56%)
  blocking collectives  10.2 us (17%)
  Pallas kernels  9.13 us (15%)
  waiting for transfers between devices  4.33 us (7%)
  local copies, waits for them, and re-layouts  1.3 us (2%)
  between operations  0.75 us (1%)
    all_to_all x2, starting transfers between devices, exchange(): lax.all_to_all(messages, 'inst', split_axis=0, concat_axis=0, axis_index_...  29.8 us
    all_to_all x1, blocking collectives, on_device(): lax.all_to_all(attended, 'tp', split_axis=0, concat_axis=0, axis_index_gr...  10.2 us
    all_to_all x2, waiting for transfers between devices, exchange(): lax.all_to_all(messages, 'inst', split_axis=0, concat_axis=0, axis_index_...  4.33 us
    ppermute x1, starting transfers between devices, on_device(): moved = lax.ppermute(leaving, 'inst', swap)  3.31 us
    pallas_call x1, Pallas kernels, resident(): pl.pallas_call(resident_kernel, out_shape=jax.ShapeDtypeStruct((rows, 2 *...  3.29 us
    pallas_call x1, Pallas kernels, pack(): pl.pallas_call(pack_kernel, out_shape=[jax.ShapeDtypeStruct((size, HD), j...  1.85 us
    pallas_call x1, Pallas kernels, prepare(): pl.pallas_call(prepare_kernel, out_shape=[paired, paired, jax.ShapeDtypeS...  1.76 us
    pallas_call x1, Pallas kernels, owner(): pl.pallas_call(owner_kernel, out_shape=jax.ShapeDtypeStruct(arrived.shape...  1.75 us
  transfers between devices with their start and end apart: 3, of which 2 were waited for; matrix products, arithmetic and copies ran while one was open for 0% of the time, Pallas kernels for 12%

profile of v1, /device:TPU:1, one launch (start us, length us, event | category | flops | bytes accessed | tf_op | source)
XLA Modules:
  0.0 58.8 jit_solution(12329209618134647040)
XLA Ops:
  0.0 0.0 copy-start.3
  0.0 1.9 %pack.1 = (bf16[1152,128]{1,0:T(8,128)(2,1)}, bf16[64,128]{1,0:T(8,128)(2,1)S(1)}) custom-call(s32[8,16]{1,0:T(8,128)} %prefix.1, bf16[8,1024]{1,0:T(8,128)(2,1)} %queries_hbm.1), custom_call_target="tpu_custom_call" | custom-call | flops 4194304 | bytes 524288 | tf_op jit(solution)/shard_map/pack/pallas_call | solution.py:94
  1.9 18.5 %all-to-all-start = ((bf16[64,9,2,128]{3,2,1,0:T(2,128)(2,1)}), bf16[64,9,2,128]{3,2,1,0:T(2,128)(2,1)S(1)}, u32[]{:S(2)}, u32[]{:S(2)}) async-start(bf16[64,9,2,128]{3,2,1,0:T(2,128)(2,1)} %bitcast), calls=%async_computation | async-start | bytes 589824 | tf_op jit(solution)/shard_map/all_to_all | solution.py:395
  21.1 0.0 copy-start.2
  21.1 0.6 %copy-done.2 = s32[8]{0:T(128)S(1)} copy-done((s32[8]{0:T(128)S(1)}, s32[8]{0:T(128)}, u32[]{:S(2)}) %copy-start.2) | copy-done | bytes 56
  21.7 1.8 %prepare.1 = (bf16[512,256]{1,0:T(8,128)(2,1)S(1)}, bf16[512,256]{1,0:T(8,128)(2,1)S(1)}, bf16[1040,256]{1,0:T(8,128)(2,1)S(1)}) custom-call(s32[1]{0:T(128)S(6)} %copy.8.mig, s32[8]{0:T(128)S(1)} %copy-done.2, bf16[1024,256]{1,0:T(8,128)(2,1)} %bitcast.11, bf16[8,1024,256]{2,1,0:T(8,128)(2,1)} %cache_hbm.3), custom_call_target="tpu_custom_call" | custom-call | bytes 1048576 | tf_op jit(solution)/shard_map/prepare/pallas_call | solution.py:158
  23.5 3.3 %collective-permute-start = (bf16[1040,256]{1,0:T(8,128)(2,1)S(1)}, bf16[1040,256]{1,0:T(8,128)(2,1)S(1)}, u32[]{:S(2)}, u32[]{:S(2)}) collective-permute-start(bf16[1040,256]{1,0:T(8,128)(2,1)S(1)} %get-tuple-element.14), channel_id=1, source_target_pairs={{0,256},{8,264},{16,272},{24,280},{32,288},{40,296},{48,304},{56,3... | collective-permute-start | bytes 1597448 | tf_op jit(solution)/shard_map/ppermute | solution.py:403
  26.8 0.6 %all-to-all-done = bf16[64,9,2,128]{3,2,1,0:T(2,128)(2,1)S(1)} async-done(((bf16[64,9,2,128]{3,2,1,0:T(2,128)(2,1)}), bf16[64,9,2,128]{3,2,1,0:T(2,128)(2,1)S(1)}, u32[]{:S(2)}, u32[]{:S(2)}) %all-to-all-start) | async-done | bytes 294944 | tf_op jit(solution)/shard_map/all_to_all | solution.py:395
  27.4 1.8 %owner.1 = bf16[1152,128]{1,0:T(8,128)(2,1)} custom-call(bf16[1152,128]{1,0:T(8,128)(2,1)S(1)} %bitcast.8, bf16[512,256]{1,0:T(8,128)(2,1)S(1)} %get-tuple-element.11.keys, bf16[512,256]{1,0:T(8,128)(2,1)S(1)} %get-tuple-element.12.values), custom_call_target="tpu_custom_call" | custom-call | flops 536870912 | bytes 2097152 | tf_op jit(solution)/shard_map/owner/pallas_call | solution.py:305
  29.2 11.2 %all-to-all-start.1 = ((bf16[64,9,2,128]{3,2,1,0:T(2,128)(2,1)}), bf16[64,9,2,128]{3,2,1,0:T(2,128)(2,1)S(1)}, u32[]{:S(2)}, u32[]{:S(2)}) async-start(bf16[64,9,2,128]{3,2,1,0:T(2,128)(2,1)} %bitcast.3), calls=%async_computation.1 | async-start | bytes 589824 | tf_op jit(solution)/shard_map/all_to_all | solution.py:395
  40.4 0.0 collective-permute-done.moved
  40.4 0.0 copy-done.3
  40.4 0.0 copy-start
  40.5 0.0 copy-start.1
  40.5 3.3 %resident.1.own = f32[8,16,128]{2,1,0:T(8,128)S(1)} custom-call(s32[1]{0:T(128)S(6)} %copy.8.mig, s32[8]{0:T(128)S(1)} %copy-done.3, bf16[8,8,128]{2,1,0:T(8,128)(2,1)S(1)} %bitcast.10, bf16[8,256]{1,0:T(8,128)(2,1)} %new_kv.1, bf16[1040,256]{1,0:T(8,128)(2,1)S(1)} %collective-permute-done.moved, bf16[8,1024,256]{2,1,0:T(8,128)(2,1)} %cache_hbm.3), custom_call_target="tpu_custom_call" | custom-call | flops 17179869184 | bytes 67108864 | tf_op jit(solution)/shard_map/resident/pallas_call | solution.py:212
  43.8 3.7 %all-to-all-done.1 = bf16[64,9,2,128]{3,2,1,0:T(2,128)(2,1)S(1)} async-done(((bf16[64,9,2,128]{3,2,1,0:T(2,128)(2,1)}), bf16[64,9,2,128]{3,2,1,0:T(2,128)(2,1)S(1)}, u32[]{:S(2)}, u32[]{:S(2)}) %all-to-all-start.1) | async-done | bytes 294944 | tf_op jit(solution)/shard_map/all_to_all | solution.py:395
  47.5 0.0 copy-done
  47.5 0.0 copy-done.1
  47.5 0.5 combine.1
  48.0 10.2 %all_to_all.15 = bf16[8,8,128]{2,1,0:T(8,128)(2,1)S(1)} all-to-all(bf16[8,8,128]{2,1,0:T(8,128)(2,1)S(1)} %bitcast.9), channel_id=1, replica_groups={{4,5,6,7,0,1,2,3},{12,13,14,15,8,9,10,11},{20,21,22,23,16,17,18,19},{28..., dimensions={0} | all-to-all | bytes 32768 | tf_op jit(solution)/shard_map/all_to_all | solution.py:409
  58.2 0.6 %reshape.31 = bf16[1,8192]{1,0:T(2,128)(2,1)} reshape(bf16[8,8,128]{2,1,0:T(8,128)(2,1)S(1)} %pad_maximum_fusion) | data formatting | bytes 32768 | tf_op jit(solution)/shard_map/reshape | solution.py:413
  (2 shorter events, 0.0 us)
Async XLA Ops:
  0.0 40.4 %copy-start.3 = (s32[8]{0:T(128)S(1)}, s32[8]{0:T(128)}, u32[]{:S(2)}) copy-start(s32[8]{0:T(128)} %lengths.3) | copy-start | bytes 100
  1.9 25.6 %all-to-all-start = ((bf16[64,9,2,128]{3,2,1,0:T(2,128)(2,1)}), bf16[64,9,2,128]{3,2,1,0:T(2,128)(2,1)S(1)}, u32[]{:S(2)}, u32[]{:S(2)}) async-start(bf16[64,9,2,128]{3,2,1,0:T(2,128)(2,1)} %bitcast), calls=%async_computation | async-start | bytes 589824 | tf_op jit(solution)/shard_map/all_to_all | solution.py:395
  21.1 0.7 %copy-start.2 = (s32[8]{0:T(128)S(1)}, s32[8]{0:T(128)}, u32[]{:S(2)}) copy-start(s32[8]{0:T(128)} %lengths.3) | copy-start | bytes 100
  23.5 16.9 %collective-permute-start = (bf16[1040,256]{1,0:T(8,128)(2,1)S(1)}, bf16[1040,256]{1,0:T(8,128)(2,1)S(1)}, u32[]{:S(2)}, u32[]{:S(2)}) collective-permute-start(bf16[1040,256]{1,0:T(8,128)(2,1)S(1)} %get-tuple-element.14), channel_id=1, source_target_pairs={{0,256},{8,264},{16,272},{24,280},{32,288},{40,296},{48,304},{56,3... | collective-permute-start | bytes 1597448 | tf_op jit(solution)/shard_map/ppermute | solution.py:403
  29.2 18.3 %all-to-all-start.1 = ((bf16[64,9,2,128]{3,2,1,0:T(2,128)(2,1)}), bf16[64,9,2,128]{3,2,1,0:T(2,128)(2,1)S(1)}, u32[]{:S(2)}, u32[]{:S(2)}) async-start(bf16[64,9,2,128]{3,2,1,0:T(2,128)(2,1)} %bitcast.3), calls=%async_computation.1 | async-start | bytes 589824 | tf_op jit(solution)/shard_map/all_to_all | solution.py:395
  40.4 7.0 %copy-start = (s32[8,16]{1,0:T(8,128)S(1)}, s32[8,16]{1,0:T(8,128)}, u32[]{:S(2)}) copy-start(s32[8,16]{1,0:T(8,128)} %prefix.1) | copy-start | bytes 1540
  40.5 7.0 %copy-start.1 = (bf16[8,256]{1,0:T(8,128)(2,1)S(1)}, bf16[8,256]{1,0:T(8,128)(2,1)}, u32[]{:S(2)}) copy-start(bf16[8,256]{1,0:T(8,128)(2,1)} %new_kv.1) | copy-start | bytes 12292

commit v2 on v1

--- a/solution.py
+++ b/solution.py
@@ -12,7 +12,7 @@
 GRP = QH // KVH
 CAP = 2
 NONE = 8191
-FIRST = 20
+FIRST = 22
 FIRST_TP = 4
 TAIL = 16
 HEADS = 2
@@ -125,28 +125,31 @@
     return mixes, stats
 
 
-def prepare_kernel(mig, lengths, pool_hbm, cache_hbm, keys, values, leaving, pool, sems):
-    tokens = cache_hbm.shape[1]
-    fetch_pool = pltpu.make_async_copy(pool_hbm, pool, sems.at[0])
-    fetch_row = pltpu.make_async_copy(
-        cache_hbm.at[mig[0]], leaving.at[pl.ds(0, tokens)], sems.at[1]
-    )
-    fetch_pool.start()
-    fetch_row.start()
+def prepare_kernel(mig, lengths_hbm, pool, cache, keys, values, leaving, lengths, sems):
+    tokens = cache.shape[1]
+    fetches = [
+        (cache.at[mig[0]], leaving.at[pl.ds(0, tokens)]),
+        (lengths_hbm, lengths),
+    ]
+    half = keys.shape[0] // BLK
+    for b in range(2):
+        lanes_of = pl.ds(b * HD, HD)
+        part = pl.ds(b * half * BLK, half * BLK)
+        fetches.append((pool.at[part, pl.ds(HD, HD)], values.at[:, lanes_of]))
+        for p in range(half):
+            block = pl.ds((2 * p + b) * BLK, BLK)
+            fetches.append((pool.at[block, pl.ds(0, HD)], keys.at[pl.ds(p * BLK, BLK), lanes_of]))
+    fetches = [pltpu.make_async_copy(*ends, sems.at[n]) for n, ends in enumerate(fetches)]
+    for fetch in fetches:
+        fetch.start()
+    fetches[1].wait()
     length = lengths[mig[0]]
     lane = lanes((TAIL, leaving.shape[1]))
     tail = jnp.where(lane == 0, length >> 3, jnp.where(lane == 1, length & 7, 0))
     leaving[tokens:] = tail.astype(jnp.float32).astype(jnp.bfloat16)
-    fetch_pool.wait()
-    half = pool.shape[0] // BLK // 2
-    for p in range(half):
-        for b in range(2):
-            block = slice((2 * p + b) * BLK, (2 * p + b + 1) * BLK)
-            keys[p * BLK : (p + 1) * BLK, b * HD : (b + 1) * HD] = pool[block, :HD]
-    for b in range(2):
-        part = slice(b * half * BLK, (b + 1) * half * BLK)
-        values[:, b * HD : (b + 1) * HD] = pool[part, HD:]
-    fetch_row.wait()
+    fetches[0].wait()
+    for fetch in fetches[2:]:
+        fetch.wait()
 
 
 def prepare(mig, lengths, pool, cache):
@@ -158,15 +161,18 @@
     return pl.pallas_call(
         prepare_kernel,
         out_shape=[paired, paired, jax.ShapeDtypeStruct((tokens + TAIL, width), cache.dtype)],
-        in_specs=[smem, smem, hbm, hbm],
+        in_specs=[smem, hbm, hbm, hbm],
         out_specs=[vmem, vmem, vmem],
-        scratch_shapes=[pltpu.VMEM(pool.shape, pool.dtype), pltpu.SemaphoreType.DMA((2,))],
+        scratch_shapes=[
+            pltpu.SMEM(lengths.shape, lengths.dtype),
+            pltpu.SemaphoreType.DMA((4 + pool.shape[0] // BLK,)),
+        ],
         compiler_params=pltpu.CompilerParams(vmem_limit_bytes=8 * MIB),
         cost_estimate=pl.CostEstimate(
             flops=0, bytes_accessed=2 * (pool.size + tokens * width), transcendentals=0
         ),
         name="prepare",
-    )(mig, lengths, in_hbm(pool), in_hbm(cache))
+    )(mig, in_hbm(lengths), in_hbm(pool), in_hbm(cache))
 
 
 def resident_kernel(

time: 59.2 us -> 59.7 us (level)
  waiting for transfers between devices: 4.33 us -> 6.8 us
  starting transfers between devices: 33.1 us -> 30.8 us
  blocking collectives: 10.2 us -> 11.5 us
  local copies, waits for them, and re-layouts: 1.3 us -> 0.65 us
    all_to_all x2, waiting for transfers between devices: 4.33 us -> 6.79 us  [exchange(): lax.all_to_all(messages, 'inst', split_axis=0, concat_axis=0, axis_index_...]
    all_to_all x2, starting transfers between devices: 29.8 us -> 27.5 us  [exchange(): lax.all_to_all(messages, 'inst', split_axis=0, concat_axis=0, axis_index_...]
    all_to_all x1, blocking collectives: 10.2 us -> 11.5 us  [on_device(): lax.all_to_all(attended, 'tp', split_axis=0, concat_axis=0, axis_index_gr...]
    unnamed x8 -> x6, local copies, waits for them, and re-layouts: 0.67 us -> 0.02 us
  transfers between devices with their start and end apart: 3 -> 3, of which waited for: 2 -> 2; matrix products, arithmetic and copies ran while one was open for 0% -> 0% of each run, Pallas kernels for 12% -> 11%
where the time goes in v2:
time: 59.7 us; the launch traced here: 59.3 us
  starting transfers between devices  30.8 us (52%)
  blocking collectives  11.5 us (19%)
  Pallas kernels  8.8 us (15%)
  waiting for transfers between devices  6.8 us (11%)
  between operations  0.74 us (1%)
  local copies, waits for them, and re-layouts  0.65 us (1%)
    all_to_all x2, starting transfers between devices, exchange(): lax.all_to_all(messages, 'inst', split_axis=0, concat_axis=0, axis_index_...  27.5 us
    all_to_all x1, blocking collectives, on_device(): lax.all_to_all(attended, 'tp', split_axis=0, concat_axis=0, axis_index_gr...  11.5 us
    all_to_all x2, waiting for transfers between devices, exchange(): lax.all_to_all(messages, 'inst', split_axis=0, concat_axis=0, axis_index_...  6.79 us
    pallas_call x1, Pallas kernels, resident(): pl.pallas_call(resident_kernel, out_shape=jax.ShapeDtypeStruct((rows, 2 *...  3.42 us
    ppermute x1, starting transfers between devices, on_device(): moved = lax.ppermute(leaving, 'inst', swap)  3.31 us
    pallas_call x1, Pallas kernels, pack(): pl.pallas_call(pack_kernel, out_shape=[jax.ShapeDtypeStruct((size, HD), j...  1.86 us
    pallas_call x1, Pallas kernels, owner(): pl.pallas_call(owner_kernel, out_shape=jax.ShapeDtypeStruct(arrived.shape...  1.76 us
    pallas_call x1, Pallas kernels, prepare(): pl.pallas_call(prepare_kernel, out_shape=[paired, paired, jax.ShapeDtypeS...  1.28 us
  transfers between devices with their start and end apart: 3, of which 2 were waited for; matrix products, arithmetic and copies ran while one was open for 0% of the time, Pallas kernels for 11%

profile of v2, /device:TPU:1, one launch (start us, length us, event | category | flops | bytes accessed | tf_op | source)
XLA Modules:
  0.0 59.3 jit_solution(18369627410633915808)
XLA Ops:
  0.0 0.0 copy-start.2
  0.0 1.9 %pack.1 = (bf16[1152,128]{1,0:T(8,128)(2,1)}, bf16[64,128]{1,0:T(8,128)(2,1)S(1)}) custom-call(s32[8,16]{1,0:T(8,128)} %prefix.1, bf16[8,1024]{1,0:T(8,128)(2,1)} %queries_hbm.1), custom_call_target="tpu_custom_call" | custom-call | flops 4194304 | bytes 524288 | tf_op jit(solution)/shard_map/pack/pallas_call | solution.py:94
  1.9 16.8 %all-to-all-start = ((bf16[64,9,2,128]{3,2,1,0:T(2,128)(2,1)}), bf16[64,9,2,128]{3,2,1,0:T(2,128)(2,1)S(1)}, u32[]{:S(2)}, u32[]{:S(2)}) async-start(bf16[64,9,2,128]{3,2,1,0:T(2,128)(2,1)} %bitcast), calls=%async_computation | async-start | bytes 589824 | tf_op jit(solution)/shard_map/all_to_all | solution.py:401
  19.3 1.3 %prepare.1 = (bf16[512,256]{1,0:T(8,128)(2,1)S(1)}, bf16[512,256]{1,0:T(8,128)(2,1)S(1)}, bf16[1040,256]{1,0:T(8,128)(2,1)S(1)}) custom-call(s32[1]{0:T(128)S(6)} %copy.8.mig, s32[8]{0:T(128)} %lengths.1, bf16[1024,256]{1,0:T(8,128)(2,1)} %bitcast.11, bf16[8,1024,256]{2,1,0:T(8,128)(2,1)} %cache_hbm.1), custom_call_target="tpu_custom_call" | custom-call | bytes 1048576 | tf_op jit(solution)/shard_map/prepare/pallas_call | solution.py:161
  20.6 3.3 %collective-permute-start = (bf16[1040,256]{1,0:T(8,128)(2,1)S(1)}, bf16[1040,256]{1,0:T(8,128)(2,1)S(1)}, u32[]{:S(2)}, u32[]{:S(2)}) collective-permute-start(bf16[1040,256]{1,0:T(8,128)(2,1)S(1)} %get-tuple-element.14), channel_id=1, source_target_pairs={{0,256},{8,264},{16,272},{24,280},{32,288},{40,296},{48,304},{56,3... | collective-permute-start | bytes 1597448 | tf_op jit(solution)/shard_map/ppermute | solution.py:409
  23.9 2.5 %all-to-all-done = bf16[64,9,2,128]{3,2,1,0:T(2,128)(2,1)S(1)} async-done(((bf16[64,9,2,128]{3,2,1,0:T(2,128)(2,1)}), bf16[64,9,2,128]{3,2,1,0:T(2,128)(2,1)S(1)}, u32[]{:S(2)}, u32[]{:S(2)}) %all-to-all-start) | async-done | bytes 294944 | tf_op jit(solution)/shard_map/all_to_all | solution.py:401
  26.4 1.8 %owner.1 = bf16[1152,128]{1,0:T(8,128)(2,1)} custom-call(bf16[1152,128]{1,0:T(8,128)(2,1)S(1)} %bitcast.8, bf16[512,256]{1,0:T(8,128)(2,1)S(1)} %get-tuple-element.11.keys, bf16[512,256]{1,0:T(8,128)(2,1)S(1)} %get-tuple-element.12.values), custom_call_target="tpu_custom_call" | custom-call | flops 536870912 | bytes 2097152 | tf_op jit(solution)/shard_map/owner/pallas_call | solution.py:311
  28.2 10.7 %all-to-all-start.1 = ((bf16[64,9,2,128]{3,2,1,0:T(2,128)(2,1)}), bf16[64,9,2,128]{3,2,1,0:T(2,128)(2,1)S(1)}, u32[]{:S(2)}, u32[]{:S(2)}) async-start(bf16[64,9,2,128]{3,2,1,0:T(2,128)(2,1)} %bitcast.3), calls=%async_computation.1 | async-start | bytes 589824 | tf_op jit(solution)/shard_map/all_to_all | solution.py:401
  38.9 0.0 collective-permute-done.moved
  38.9 0.0 copy-done.2
  38.9 0.0 copy-start
  38.9 0.0 copy-start.1
  38.9 3.4 %resident.1.own = f32[8,16,128]{2,1,0:T(8,128)S(1)} custom-call(s32[1]{0:T(128)S(6)} %copy.8.mig, s32[8]{0:T(128)S(1)} %copy-done.2, bf16[8,8,128]{2,1,0:T(8,128)(2,1)S(1)} %bitcast.10, bf16[8,256]{1,0:T(8,128)(2,1)} %new_kv.1, bf16[1040,256]{1,0:T(8,128)(2,1)S(1)} %collective-permute-done.moved, bf16[8,1024,256]{2,1,0:T(8,128)(2,1)} %cache_hbm.1), custom_call_target="tpu_custom_call" | custom-call | flops 17179869184 | bytes 67108864 | tf_op jit(solution)/shard_map/resident/pallas_call | solution.py:218
  42.3 4.3 %all-to-all-done.1 = bf16[64,9,2,128]{3,2,1,0:T(2,128)(2,1)S(1)} async-done(((bf16[64,9,2,128]{3,2,1,0:T(2,128)(2,1)}), bf16[64,9,2,128]{3,2,1,0:T(2,128)(2,1)S(1)}, u32[]{:S(2)}, u32[]{:S(2)}) %all-to-all-start.1) | async-done | bytes 294944 | tf_op jit(solution)/shard_map/all_to_all | solution.py:401
  46.6 0.0 copy-done
  46.6 0.0 copy-done.1
  46.6 0.5 combine.1
  47.1 11.5 %all_to_all.15 = bf16[8,8,128]{2,1,0:T(8,128)(2,1)S(1)} all-to-all(bf16[8,8,128]{2,1,0:T(8,128)(2,1)S(1)} %bitcast.9), channel_id=1, replica_groups={{4,5,6,7,0,1,2,3},{12,13,14,15,8,9,10,11},{20,21,22,23,16,17,18,19},{28..., dimensions={0} | all-to-all | bytes 32768 | tf_op jit(solution)/shard_map/all_to_all | solution.py:415
  58.6 0.6 %reshape.31 = bf16[1,8192]{1,0:T(2,128)(2,1)} reshape(bf16[8,8,128]{2,1,0:T(8,128)(2,1)S(1)} %pad_maximum_fusion) | data formatting | bytes 32768 | tf_op jit(solution)/shard_map/reshape | solution.py:419
  (2 shorter events, 0.0 us)
Async XLA Ops:
  0.0 38.9 %copy-start.2 = (s32[8]{0:T(128)S(1)}, s32[8]{0:T(128)}, u32[]{:S(2)}) copy-start(s32[8]{0:T(128)} %lengths.1) | copy-start | bytes 100
  1.9 24.5 %all-to-all-start = ((bf16[64,9,2,128]{3,2,1,0:T(2,128)(2,1)}), bf16[64,9,2,128]{3,2,1,0:T(2,128)(2,1)S(1)}, u32[]{:S(2)}, u32[]{:S(2)}) async-start(bf16[64,9,2,128]{3,2,1,0:T(2,128)(2,1)} %bitcast), calls=%async_computation | async-start | bytes 589824 | tf_op jit(solution)/shard_map/all_to_all | solution.py:401
  20.6 18.3 %collective-permute-start = (bf16[1040,256]{1,0:T(8,128)(2,1)S(1)}, bf16[1040,256]{1,0:T(8,128)(2,1)S(1)}, u32[]{:S(2)}, u32[]{:S(2)}) collective-permute-start(bf16[1040,256]{1,0:T(8,128)(2,1)S(1)} %get-tuple-element.14), channel_id=1, source_target_pairs={{0,256},{8,264},{16,272},{24,280},{32,288},{40,296},{48,304},{56,3... | collective-permute-start | bytes 1597448 | tf_op jit(solution)/shard_map/ppermute | solution.py:409
  28.2 18.5 %all-to-all-start.1 = ((bf16[64,9,2,128]{3,2,1,0:T(2,128)(2,1)}), bf16[64,9,2,128]{3,2,1,0:T(2,128)(2,1)S(1)}, u32[]{:S(2)}, u32[]{:S(2)}) async-start(bf16[64,9,2,128]{3,2,1,0:T(2,128)(2,1)} %bitcast.3), calls=%async_computation.1 | async-start | bytes 589824 | tf_op jit(solution)/shard_map/all_to_all | solution.py:401
  38.9 7.7 %copy-start = (s32[8,16]{1,0:T(8,128)S(1)}, s32[8,16]{1,0:T(8,128)}, u32[]{:S(2)}) copy-start(s32[8,16]{1,0:T(8,128)} %prefix.1) | copy-start | bytes 1540
  38.9 7.7 %copy-start.1 = (bf16[8,256]{1,0:T(8,128)(2,1)S(1)}, bf16[8,256]{1,0:T(8,128)(2,1)}, u32[]{:S(2)}) copy-start(bf16[8,256]{1,0:T(8,128)(2,1)} %new_kv.1) | copy-start | bytes 12292

commit v3 on v2

--- a/solution.py
+++ b/solution.py
@@ -12,7 +12,7 @@
 GRP = QH // KVH
 CAP = 2
 NONE = 8191
-FIRST = 22
+FIRST = 20
 FIRST_TP = 4
 TAIL = 16
 HEADS = 2
@@ -57,16 +57,29 @@
     return jnp.where(lanes((1, slots)) < insts, first, second)
 
 
-def pack_kernel(prefix_hbm, queries_hbm, out, heads, stage, flat, prefix, queries, sems):
+def send_out(put, insts, stage, packed, out, sems):
+    half = insts // 2
+    copies = []
+    for h in range(2):
+        for r, part in put:
+            first = h * half * ROWS + r
+            stage[pl.ds(first, half, stride=ROWS), :] = part[h * half : (h + 1) * half]
+        span = pl.ds(h * half * ROWS, half * ROWS)
+        packed[span, :] = stage[span, :].astype(jnp.bfloat16)
+        copies.append(pltpu.make_async_copy(packed.at[span], out.at[span], sems.at[h]))
+        copies[h].start()
+    for copy in copies:
+        copy.wait()
+
+
+def pack_kernel(prefix_hbm, queries_hbm, out, stage, packed, prefix, queries, sems, out_sems):
     fetch_prefix = pltpu.make_async_copy(prefix_hbm, prefix, sems.at[0])
     fetch_queries = pltpu.make_async_copy(queries_hbm, queries, sems.at[1])
     fetch_prefix.start()
     fetch_queries.start()
     insts = stage.shape[0] // ROWS
-    for r in range(CAP * GRP + 1, ROWS):
-        stage[pl.ds(r, insts, stride=ROWS), :] = jnp.zeros((insts, HD), jnp.float32)
+    slots = CAP * insts
     fetch_prefix.wait()
-    slots = CAP * insts
     codes = jnp.broadcast_to(slot_codes(prefix[...], insts), (slots, slots)).T.astype(jnp.int32)
     pick = ((codes >> 7) == lanes(codes.shape))[:, :GRP].astype(jnp.float32).astype(jnp.bfloat16)
     fetch_queries.wait()
@@ -74,36 +87,30 @@
     lane = lanes((insts, HD))
     local = (codes & 7).astype(jnp.float32)
     ids = jnp.where(lane == 0, local[:insts], jnp.where(lane == 1, local[insts:], 0.0))
-    for k in range(CAP):
-        for g in range(GRP):
-            part = picked[k * insts : (k + 1) * insts, g * HD : (g + 1) * HD]
-            stage[pl.ds(k * GRP + g, insts, stride=ROWS), :] = part
-    stage[pl.ds(CAP * GRP, insts, stride=ROWS), :] = ids
-    out[...] = stage[...].astype(jnp.bfloat16)
-    own = queries[...].astype(jnp.float32)
-    for g in range(GRP):
-        flat[pl.ds(g, own.shape[0], stride=GRP), :] = own[:, g * HD : (g + 1) * HD]
-    heads[...] = flat[...].astype(jnp.bfloat16)
+    put = [
+        (k * GRP + g, picked[k * insts : (k + 1) * insts, g * HD : (g + 1) * HD])
+        for k in range(CAP)
+        for g in range(GRP)
+    ]
+    put.append((CAP * GRP, ids))
+    put.append((CAP * GRP + 1, jnp.zeros((insts, HD), jnp.float32)))
+    send_out(put, insts, stage, packed, out, out_sems)
 
 
 def pack(insts, prefix, queries):
     size = insts * ROWS
-    flat = queries.shape[0] * GRP
     hbm = pl.BlockSpec(memory_space=pltpu.HBM)
-    vmem = pl.BlockSpec(memory_space=pltpu.VMEM)
     return pl.pallas_call(
         pack_kernel,
-        out_shape=[
-            jax.ShapeDtypeStruct((size, HD), jnp.bfloat16),
-            jax.ShapeDtypeStruct((flat, HD), jnp.bfloat16),
-        ],
+        out_shape=jax.ShapeDtypeStruct((size, HD), jnp.bfloat16),
         in_specs=[hbm, hbm],
-        out_specs=[vmem, vmem],
+        out_specs=pl.BlockSpec(memory_space=pl.ANY),
         scratch_shapes=[
             pltpu.VMEM((size, HD), jnp.float32),
-            pltpu.VMEM((flat, HD), jnp.float32),
+            pltpu.VMEM((size, HD), jnp.bfloat16),
             pltpu.VMEM(prefix.shape, prefix.dtype),
             pltpu.VMEM(queries.shape, queries.dtype),
+            pltpu.SemaphoreType.DMA((2,)),
             pltpu.SemaphoreType.DMA((2,)),
         ],
         compiler_params=pltpu.CompilerParams(vmem_limit_bytes=8 * MIB),
@@ -176,13 +183,34 @@
 
 
 def resident_kernel(
-    mig, lengths, query, new_kv_hbm, moved, cache_hbm, out, cache, tail, new_kv, sems, sem_tail, sem_new
+    mig,
+    lengths,
+    queries_hbm,
+    new_kv_hbm,
+    prefix_hbm,
+    moved,
+    cache_hbm,
+    out,
+    belongs,
+    cache,
+    tail,
+    new_kv,
+    queries,
+    prefix,
+    flat,
+    sems,
+    small_sems,
 ):
     rows, tokens, _ = cache.shape
-    fetch_tail = pltpu.make_async_copy(moved.at[pl.ds(tokens, TAIL)], tail, sem_tail)
-    fetch_new = pltpu.make_async_copy(new_kv_hbm, new_kv, sem_new)
-    fetch_tail.start()
-    fetch_new.start()
+    small = [
+        (queries_hbm, queries),
+        (new_kv_hbm, new_kv),
+        (prefix_hbm, prefix),
+        (moved.at[pl.ds(tokens, TAIL)], tail),
+    ]
+    small = [pltpu.make_async_copy(*ends, small_sems.at[n]) for n, ends in enumerate(small)]
+    for fetch in small:
+        fetch.start()
     fetches = []
     for s in range(rows):
         here = pltpu.make_async_copy(cache_hbm.at[s], cache.at[s], sems.at[s])
@@ -190,16 +218,22 @@
         pl.when(mig[0] != s)(here.start)
         pl.when(mig[0] == s)(came.start)
         fetches.append(here)
-    fetch_tail.wait()
-    fetch_new.wait()
+    for fetch in small:
+        fetch.wait()
+    codes = slot_codes(prefix[...], belongs.shape[1] // CAP).astype(jnp.int32)
+    belongs[...] = jnp.broadcast_to(jnp.where(codes < NONE, codes >> 7, -1), belongs.shape)
     parts = tail[...].astype(jnp.float32)
     moved_length = (parts[0:1, 0:1] * 8.0 + parts[0:1, 1:2]).astype(jnp.int32)
     length = [jnp.where(mig[0] == s, moved_length, lengths[s]) for s in range(rows)]
+    own = queries[...].astype(jnp.float32)
+    for g in range(GRP):
+        flat[pl.ds(g, rows, stride=GRP), :] = own[:, g * HD : (g + 1) * HD]
+    query = [flat[s * GRP : (s + 1) * GRP, :] for s in range(rows)]
     key = new_kv[:, :HD].astype(jnp.float32)
     fresh = [
-        jnp.sum(query[s].astype(jnp.float32) * key[s : s + 1], axis=1, keepdims=True) * SCALE
-        for s in range(rows)
-    ]
+        jnp.sum(query[s] * key[s : s + 1], axis=1, keepdims=True) * SCALE for s in range(rows)
+    ]
+    query = [q.astype(jnp.bfloat16) for q in query]
     for c in range(0, rows, TOGETHER):
         slots = range(c, c + TOGETHER)
         for s in slots:
@@ -210,33 +244,38 @@
             out[s, GRP:] = jnp.where(lanes((GRP, HD)) == 2, fresh[s], stat)
 
 
-def resident(mig, lengths, query, new_kv, moved, cache):
+def resident(insts, mig, lengths, queries, new_kv, prefix, moved, cache):
     rows, tokens, width = cache.shape
     smem = pl.BlockSpec(memory_space=pltpu.SMEM)
     vmem = pl.BlockSpec(memory_space=pltpu.VMEM)
     hbm = pl.BlockSpec(memory_space=pltpu.HBM)
     return pl.pallas_call(
         resident_kernel,
-        out_shape=jax.ShapeDtypeStruct((rows, 2 * GRP, HD), jnp.float32),
-        in_specs=[smem, smem, vmem, hbm, pl.BlockSpec(memory_space=pl.ANY), hbm],
-        out_specs=vmem,
+        out_shape=[
+            jax.ShapeDtypeStruct((rows, 2 * GRP, HD), jnp.float32),
+            jax.ShapeDtypeStruct((GRP, CAP * insts), jnp.int32),
+        ],
+        in_specs=[smem, smem, hbm, hbm, hbm, pl.BlockSpec(memory_space=pl.ANY), hbm],
+        out_specs=[vmem, vmem],
         scratch_shapes=[
             pltpu.VMEM(cache.shape, cache.dtype),
             pltpu.VMEM((TAIL, width), cache.dtype),
             pltpu.VMEM(new_kv.shape, new_kv.dtype),
+            pltpu.VMEM(queries.shape, queries.dtype),
+            pltpu.VMEM(prefix.shape, prefix.dtype),
+            pltpu.VMEM((rows * GRP, HD), jnp.float32),
             pltpu.SemaphoreType.DMA((rows,)),
-            pltpu.SemaphoreType.DMA,
-            pltpu.SemaphoreType.DMA,
+            pltpu.SemaphoreType.DMA((4,)),
         ],
         compiler_params=pltpu.CompilerParams(vmem_limit_bytes=12 * MIB),
         cost_estimate=pl.CostEstimate(
             flops=1 << 34, bytes_accessed=1 << 26, transcendentals=rows * GRP * tokens
         ),
         name="resident",
-    )(mig, lengths, query, in_hbm(new_kv), moved, in_hbm(cache))
-
-
-def owner_kernel(arrived, keys, values, out, stage):
+    )(mig, lengths, in_hbm(queries), in_hbm(new_kv), in_hbm(prefix), moved, in_hbm(cache))
+
+
+def owner_kernel(arrived, keys, values, out, stage, packed, sems):
     stage[...] = arrived[...].astype(jnp.float32)
     insts = stage.shape[0] // ROWS
     slots = CAP * insts
@@ -297,13 +336,13 @@
             stats = jnp.where(lane == 2 * GRP + g, total_lo[part], stats)
         scores, waiting = following, spread
     mixes.append(mix(waiting))
+    put = []
     for k in range(CAP):
         for g in range(GRP):
             start = g % HEADS * slots + k * insts
-            part = mixes[g // HEADS][start : start + insts]
-            stage[pl.ds(k * GRP + g, insts, stride=ROWS), :] = part
-        stage[pl.ds(CAP * GRP + k, insts, stride=ROWS), :] = stats[k * insts : (k + 1) * insts]
-    out[...] = stage[...].astype(jnp.bfloat16)
+            put.append((k * GRP + g, mixes[g // HEADS][start : start + insts]))
+        put.append((CAP * GRP + k, stats[k * insts : (k + 1) * insts]))
+    send_out(put, insts, stage, packed, out, sems)
 
 
 def owner(arrived, keys, values):
@@ -312,8 +351,12 @@
         owner_kernel,
         out_shape=jax.ShapeDtypeStruct(arrived.shape, jnp.bfloat16),
         in_specs=[vmem, vmem, vmem],
-        out_specs=vmem,
-        scratch_shapes=[pltpu.VMEM(arrived.shape, jnp.float32)],
+        out_specs=pl.BlockSpec(memory_space=pl.ANY),
+        scratch_shapes=[
+            pltpu.VMEM(arrived.shape, jnp.float32),
+            pltpu.VMEM(arrived.shape, jnp.bfloat16),
+            pltpu.SemaphoreType.DMA((2,)),
+        ],
         compiler_params=pltpu.CompilerParams(vmem_limit_bytes=24 * MIB),
         cost_estimate=pl.CostEstimate(
             flops=1 << 29, bytes_accessed=2 << 20, transcendentals=1 << 17
@@ -322,13 +365,11 @@
     )(arrived, keys, values)
 
 
-def combine_kernel(prefix, arrived, own, new_kv, out, wide, table):
+def combine_kernel(belongs, arrived, own, new_kv, out, wide, table):
     wide[...] = arrived[...].astype(jnp.float32)
     insts = wide.shape[0] // ROWS
     rows = own.shape[0]
     slots = CAP * insts
-    codes = slot_codes(prefix[...], insts).astype(jnp.int32)
-    belongs = jnp.where(codes < NONE, codes >> 7, -1)
 
     def rows_of(r):
         return wide[pl.ds(r, insts, stride=ROWS), :]
@@ -339,7 +380,7 @@
     values = new_kv[:, HD:].astype(jnp.float32)
     below, mixes = [], []
     for s in range(rows):
-        mine = jnp.broadcast_to(belongs, (GRP, slots)) == s
+        mine = belongs[...] == s
         stat = own[s, GRP:]
         res_peak, res_total, new_peak = stat[:, 0:1], stat[:, 1:2], stat[:, 2:3]
         top = jnp.max(jnp.where(mine, peak, LOW), axis=1, keepdims=True)
@@ -371,7 +412,7 @@
     out[...] = jnp.concatenate(attended, axis=0).astype(jnp.bfloat16)
 
 
-def combine(prefix, arrived, own, new_kv):
+def combine(belongs, arrived, own, new_kv):
     rows = own.shape[0]
     vmem = pl.BlockSpec(memory_space=pltpu.VMEM)
     return pl.pallas_call(
@@ -386,7 +427,7 @@
         compiler_params=pltpu.CompilerParams(vmem_limit_bytes=8 * MIB),
         cost_estimate=pl.CostEstimate(flops=1 << 24, bytes_accessed=1 << 20, transcendentals=8192),
         name="combine",
-    )(prefix, arrived, own, new_kv)
+    )(belongs, arrived, own, new_kv)
 
 
 def on_device(queries, new_kv, cache, lengths, migrate_slot, pool, prefix_blocks):
@@ -403,14 +444,14 @@
         )
         return arrived.reshape(-1, HD)
 
-    messages, query = pack(insts, prefix_blocks, queries)
-    asked = exchange(messages)
+    asked = exchange(pack(insts, prefix_blocks, queries))
     keys, values, leaving = prepare(migrate_slot, lengths, pool.reshape(-1, 2 * HD), cache)
     moved = lax.ppermute(leaving, "inst", swap)
     answers = exchange(owner(asked, keys, values))
-    query = query.reshape(rows, GRP, HD)
-    own = resident(migrate_slot, lengths, query, new_kv, moved, cache)
-    attended = combine(prefix_blocks, answers, own, new_kv)
+    own, belongs = resident(
+        insts, migrate_slot, lengths, queries, new_kv, prefix_blocks, moved, cache
+    )
+    attended = combine(belongs, answers, own, new_kv)
     attended = attended.reshape(rows, GRP, HD)
     heads = lax.all_to_all(
         attended, "tp", split_axis=0, concat_axis=0, axis_index_groups=order_tp, tiled=True

time: 59.7 us -> 59.3 us (level)
  starting transfers between devices: 30.8 us -> 33.1 us
  waiting for transfers between devices: 6.8 us -> 5.3 us
  blocking collectives: 11.5 us -> 10.2 us
    all_to_all x2, starting transfers between devices: 27.5 us -> 29.8 us  [exchange(): lax.all_to_all(messages, 'inst', split_axis=0, concat_axis=0, axis_index_...]
    all_to_all x2, waiting for transfers between devices: 6.79 us -> 5.3 us  [exchange(): lax.all_to_all(messages, 'inst', split_axis=0, concat_axis=0, axis_index_...]
    all_to_all x1, blocking collectives: 11.5 us -> 10.2 us  [on_device(): lax.all_to_all(attended, 'tp', split_axis=0, concat_axis=0, axis_index_gr...]
where the time goes in v3:
time: 59.3 us; the launch traced here: 58.9 us
  starting transfers between devices  33.1 us (56%)
  blocking collectives  10.2 us (17%)
  Pallas kernels  8.9 us (15%)
  waiting for transfers between devices  5.3 us (9%)
  between operations  0.74 us (1%)
  local copies, waits for them, and re-layouts  0.64 us (1%)
    all_to_all x2, starting transfers between devices, exchange(): lax.all_to_all(messages, 'inst', split_axis=0, concat_axis=0, axis_index_...  29.8 us
    all_to_all x1, blocking collectives, on_device(): lax.all_to_all(attended, 'tp', split_axis=0, concat_axis=0, axis_index_gr...  10.2 us
    all_to_all x2, waiting for transfers between devices, exchange(): lax.all_to_all(messages, 'inst', split_axis=0, concat_axis=0, axis_index_...  5.3 us
    pallas_call x1, Pallas kernels, resident(): pl.pallas_call(resident_kernel, out_shape=[jax.ShapeDtypeStruct((rows, 2...  3.46 us
    ppermute x1, starting transfers between devices, on_device(): moved = lax.ppermute(leaving, 'inst', swap)  3.31 us
    pallas_call x1, Pallas kernels, pack(): pl.pallas_call(pack_kernel, out_shape=jax.ShapeDtypeStruct((size, HD), jn...  1.87 us
    pallas_call x1, Pallas kernels, owner(): pl.pallas_call(owner_kernel, out_shape=jax.ShapeDtypeStruct(arrived.shape...  1.77 us
    pallas_call x1, Pallas kernels, prepare(): pl.pallas_call(prepare_kernel, out_shape=[paired, paired, jax.ShapeDtypeS...  1.28 us
  transfers between devices with their start and end apart: 3, of which 2 were waited for; matrix products, arithmetic and copies ran while one was open for 0% of the time, Pallas kernels for 11%

profile of v3, /device:TPU:1, one launch (start us, length us, event | category | flops | bytes accessed | tf_op | source)
XLA Modules:
  0.0 58.9 jit_solution(9184408380646762350)
XLA Ops:
  0.0 0.0 copy-start.1
  0.0 1.9 %pack.1 = bf16[1152,128]{1,0:T(8,128)(2,1)} custom-call(s32[8,16]{1,0:T(8,128)} %prefix_hbm.3, bf16[8,1024]{1,0:T(8,128)(2,1)} %queries_hbm.3), custom_call_target="tpu_custom_call" | custom-call | flops 4194304 | bytes 524288 | tf_op jit(solution)/shard_map/pack/pallas_call | solution.py:103
  1.9 18.5 %all-to-all-start = ((bf16[64,9,2,128]{3,2,1,0:T(2,128)(2,1)}), bf16[64,9,2,128]{3,2,1,0:T(2,128)(2,1)S(1)}, u32[]{:S(2)}, u32[]{:S(2)}) async-start(bf16[64,9,2,128]{3,2,1,0:T(2,128)(2,1)} %bitcast.1), calls=%async_computation | async-start | bytes 589824 | tf_op jit(solution)/shard_map/all_to_all | solution.py:442
  21.1 1.3 %prepare.1 = (bf16[512,256]{1,0:T(8,128)(2,1)S(1)}, bf16[512,256]{1,0:T(8,128)(2,1)S(1)}, bf16[1040,256]{1,0:T(8,128)(2,1)S(1)}) custom-call(s32[1]{0:T(128)S(6)} %copy.8.mig, s32[8]{0:T(128)} %lengths.1, bf16[1024,256]{1,0:T(8,128)(2,1)} %bitcast.9, bf16[8,1024,256]{2,1,0:T(8,128)(2,1)} %cache_hbm.1), custom_call_target="tpu_custom_call" | custom-call | bytes 1048576 | tf_op jit(solution)/shard_map/prepare/pallas_call | solution.py:168
  22.4 3.3 %collective-permute-start = (bf16[1040,256]{1,0:T(8,128)(2,1)S(1)}, bf16[1040,256]{1,0:T(8,128)(2,1)S(1)}, u32[]{:S(2)}, u32[]{:S(2)}) collective-permute-start(bf16[1040,256]{1,0:T(8,128)(2,1)S(1)} %get-tuple-element.10), channel_id=1, source_target_pairs={{0,256},{8,264},{16,272},{24,280},{32,288},{40,296},{48,304},{56,3... | collective-permute-start | bytes 1597448 | tf_op jit(solution)/shard_map/ppermute | solution.py:449
  25.7 1.8 %all-to-all-done = bf16[64,9,2,128]{3,2,1,0:T(2,128)(2,1)S(1)} async-done(((bf16[64,9,2,128]{3,2,1,0:T(2,128)(2,1)}), bf16[64,9,2,128]{3,2,1,0:T(2,128)(2,1)S(1)}, u32[]{:S(2)}, u32[]{:S(2)}) %all-to-all-start) | async-done | bytes 294944 | tf_op jit(solution)/shard_map/all_to_all | solution.py:442
  27.4 1.8 %owner.1 = bf16[1152,128]{1,0:T(8,128)(2,1)} custom-call(bf16[1152,128]{1,0:T(8,128)(2,1)S(1)} %bitcast.7, bf16[512,256]{1,0:T(8,128)(2,1)S(1)} %get-tuple-element.12.keys, bf16[512,256]{1,0:T(8,128)(2,1)S(1)} %get-tuple-element.13.values), custom_call_target="tpu_custom_call" | custom-call | flops 536870912 | bytes 2097152 | tf_op jit(solution)/shard_map/owner/pallas_call | solution.py:350
  29.2 11.2 %all-to-all-start.1 = ((bf16[64,9,2,128]{3,2,1,0:T(2,128)(2,1)}), bf16[64,9,2,128]{3,2,1,0:T(2,128)(2,1)S(1)}, u32[]{:S(2)}, u32[]{:S(2)}) async-start(bf16[64,9,2,128]{3,2,1,0:T(2,128)(2,1)} %bitcast.3), calls=%async_computation.1 | async-start | bytes 589824 | tf_op jit(solution)/shard_map/all_to_all | solution.py:442
  40.5 0.0 copy-start
  40.5 0.0 collective-permute-done.moved
  40.5 0.0 copy-done.1
  40.5 3.5 %resident.1 = (f32[8,16,128]{2,1,0:T(8,128)S(1)}, s32[8,128]{1,0:T(8,128)S(1)}) custom-call(s32[1]{0:T(128)S(6)} %copy.8.mig, s32[8]{0:T(128)S(1)} %copy-done.1, bf16[8,1024]{1,0:T(8,128)(2,1)} %queries_hbm.3, bf16[8,256]{1,0:T(8,128)(2,1)} %new_kv.1, s32[8,16]{1,0:T(8,128)} %prefix_hbm.3, bf16[1040,256]{1,0:T(8,128)(2,1)S(1)} %collective-permute-done.moved, ...), custom_call_target="tpu_custom_call" | custom-call | flops 17179869184 | bytes 67108864 | tf_op jit(solution)/shard_map/resident/pallas_call | solution.py:252
  44.0 3.5 %all-to-all-done.1 = bf16[64,9,2,128]{3,2,1,0:T(2,128)(2,1)S(1)} async-done(((bf16[64,9,2,128]{3,2,1,0:T(2,128)(2,1)}), bf16[64,9,2,128]{3,2,1,0:T(2,128)(2,1)S(1)}, u32[]{:S(2)}, u32[]{:S(2)}) %all-to-all-start.1) | async-done | bytes 294944 | tf_op jit(solution)/shard_map/all_to_all | solution.py:442
  47.5 0.0 copy-done
  47.5 0.5 combine.1
  48.0 10.2 %all_to_all.15 = bf16[8,8,128]{2,1,0:T(8,128)(2,1)S(1)} all-to-all(bf16[8,8,128]{2,1,0:T(8,128)(2,1)S(1)} %bitcast.8), channel_id=1, replica_groups={{4,5,6,7,0,1,2,3},{12,13,14,15,8,9,10,11},{20,21,22,23,16,17,18,19},{28..., dimensions={0} | all-to-all | bytes 32768 | tf_op jit(solution)/shard_map/all_to_all | solution.py:456
  58.3 0.6 %reshape.27 = bf16[1,8192]{1,0:T(2,128)(2,1)} reshape(bf16[8,8,128]{2,1,0:T(8,128)(2,1)S(1)} %pad_maximum_fusion) | data formatting | bytes 32768 | tf_op jit(solution)/shard_map/reshape | solution.py:460
  (2 shorter events, 0.0 us)
Async XLA Ops:
  0.0 40.5 %copy-start.1 = (s32[8]{0:T(128)S(1)}, s32[8]{0:T(128)}, u32[]{:S(2)}) copy-start(s32[8]{0:T(128)} %lengths.1) | copy-start | bytes 100
  1.9 25.6 %all-to-all-start = ((bf16[64,9,2,128]{3,2,1,0:T(2,128)(2,1)}), bf16[64,9,2,128]{3,2,1,0:T(2,128)(2,1)S(1)}, u32[]{:S(2)}, u32[]{:S(2)}) async-start(bf16[64,9,2,128]{3,2,1,0:T(2,128)(2,1)} %bitcast.1), calls=%async_computation | async-start | bytes 589824 | tf_op jit(solution)/shard_map/all_to_all | solution.py:442
  22.4 18.1 %collective-permute-start = (bf16[1040,256]{1,0:T(8,128)(2,1)S(1)}, bf16[1040,256]{1,0:T(8,128)(2,1)S(1)}, u32[]{:S(2)}, u32[]{:S(2)}) collective-permute-start(bf16[1040,256]{1,0:T(8,128)(2,1)S(1)} %get-tuple-element.10), channel_id=1, source_target_pairs={{0,256},{8,264},{16,272},{24,280},{32,288},{40,296},{48,304},{56,3... | collective-permute-start | bytes 1597448 | tf_op jit(solution)/shard_map/ppermute | solution.py:449
  29.2 18.3 %all-to-all-start.1 = ((bf16[64,9,2,128]{3,2,1,0:T(2,128)(2,1)}), bf16[64,9,2,128]{3,2,1,0:T(2,128)(2,1)S(1)}, u32[]{:S(2)}, u32[]{:S(2)}) async-start(bf16[64,9,2,128]{3,2,1,0:T(2,128)(2,1)} %bitcast.3), calls=%async_computation.1 | async-start | bytes 589824 | tf_op jit(solution)/shard_map/all_to_all | solution.py:442
  40.5 7.0 %copy-start = (bf16[8,256]{1,0:T(8,128)(2,1)S(1)}, bf16[8,256]{1,0:T(8,128)(2,1)}, u32[]{:S(2)}) copy-start(bf16[8,256]{1,0:T(8,128)(2,1)} %new_kv.1) | copy-start | bytes 12292

commit v4 on v3

--- a/solution.py
+++ b/solution.py
@@ -15,8 +15,9 @@
 FIRST = 20
 FIRST_TP = 4
 TAIL = 16
-HEADS = 2
+HEADS = 4
 TOGETHER = 4
+SPARE = 24
 ROWS = 18
 SCALE = HD**-0.5
 LOW = -1e30
@@ -77,7 +78,7 @@
     fetch_queries = pltpu.make_async_copy(queries_hbm, queries, sems.at[1])
     fetch_prefix.start()
     fetch_queries.start()
-    insts = stage.shape[0] // ROWS
+    insts = packed.shape[0] // ROWS
     slots = CAP * insts
     fetch_prefix.wait()
     codes = jnp.broadcast_to(slot_codes(prefix[...], insts), (slots, slots)).T.astype(jnp.int32)
@@ -106,7 +107,7 @@
         in_specs=[hbm, hbm],
         out_specs=pl.BlockSpec(memory_space=pl.ANY),
         scratch_shapes=[
-            pltpu.VMEM((size, HD), jnp.float32),
+            pltpu.VMEM((size + SPARE, HD), jnp.float32),
             pltpu.VMEM((size, HD), jnp.bfloat16),
             pltpu.VMEM(prefix.shape, prefix.dtype),
             pltpu.VMEM(queries.shape, queries.dtype),
@@ -263,7 +264,7 @@
             pltpu.VMEM(new_kv.shape, new_kv.dtype),
             pltpu.VMEM(queries.shape, queries.dtype),
             pltpu.VMEM(prefix.shape, prefix.dtype),
-            pltpu.VMEM((rows * GRP, HD), jnp.float32),
+            pltpu.VMEM((rows * GRP + SPARE, HD), jnp.float32),
             pltpu.SemaphoreType.DMA((rows,)),
             pltpu.SemaphoreType.DMA((4,)),
         ],
@@ -276,8 +277,9 @@
 
 
 def owner_kernel(arrived, keys, values, out, stage, packed, sems):
-    stage[...] = arrived[...].astype(jnp.float32)
-    insts = stage.shape[0] // ROWS
+    size = arrived.shape[0]
+    stage[:size] = arrived[...].astype(jnp.float32)
+    insts = size // ROWS
     slots = CAP * insts
     half = keys.shape[0] // BLK
 
@@ -353,7 +355,7 @@
         in_specs=[vmem, vmem, vmem],
         out_specs=pl.BlockSpec(memory_space=pl.ANY),
         scratch_shapes=[
-            pltpu.VMEM(arrived.shape, jnp.float32),
+            pltpu.VMEM((arrived.shape[0] + SPARE, HD), jnp.float32),
             pltpu.VMEM(arrived.shape, jnp.bfloat16),
             pltpu.SemaphoreType.DMA((2,)),
         ],
@@ -366,8 +368,9 @@
 
 
 def combine_kernel(belongs, arrived, own, new_kv, out, wide, table):
-    wide[...] = arrived[...].astype(jnp.float32)
-    insts = wide.shape[0] // ROWS
+    size = arrived.shape[0]
+    wide[:size] = arrived[...].astype(jnp.float32)
+    insts = size // ROWS
     rows = own.shape[0]
     slots = CAP * insts
 
@@ -421,8 +424,8 @@
         in_specs=[vmem] * 4,
         out_specs=vmem,
         scratch_shapes=[
-            pltpu.VMEM(arrived.shape, jnp.float32),
-            pltpu.VMEM((rows * GRP, HD), jnp.float32),
+            pltpu.VMEM((arrived.shape[0] + SPARE, HD), jnp.float32),
+            pltpu.VMEM((rows * GRP + SPARE, HD), jnp.float32),
         ],
         compiler_params=pltpu.CompilerParams(vmem_limit_bytes=8 * MIB),
         cost_estimate=pl.CostEstimate(flops=1 << 24, bytes_accessed=1 << 20, transcendentals=8192),

time: 59.3 us -> 59.2 us (level)
  no operation moved by 1% of the time
where the time goes in v4:
time: 59.2 us; the launch traced here: 58.8 us
  starting transfers between devices  33.1 us (56%)
  blocking collectives  10.2 us (17%)
  Pallas kernels  8.71 us (15%)
  waiting for transfers between devices  5.43 us (9%)
  between operations  0.74 us (1%)
  local copies, waits for them, and re-layouts  0.64 us (1%)
    all_to_all x2, starting transfers between devices, exchange(): lax.all_to_all(messages, 'inst', split_axis=0, concat_axis=0, axis_index_...  29.8 us
    all_to_all x1, blocking collectives, on_device(): lax.all_to_all(attended, 'tp', split_axis=0, concat_axis=0, axis_index_gr...  10.2 us
    all_to_all x2, waiting for transfers between devices, exchange(): lax.all_to_all(messages, 'inst', split_axis=0, concat_axis=0, axis_index_...  5.43 us
    pallas_call x1, Pallas kernels, resident(): pl.pallas_call(resident_kernel, out_shape=[jax.ShapeDtypeStruct((rows, 2...  3.33 us
    ppermute x1, starting transfers between devices, on_device(): moved = lax.ppermute(leaving, 'inst', swap)  3.31 us
    pallas_call x1, Pallas kernels, pack(): pl.pallas_call(pack_kernel, out_shape=jax.ShapeDtypeStruct((size, HD), jn...  1.87 us
    pallas_call x1, Pallas kernels, owner(): pl.pallas_call(owner_kernel, out_shape=jax.ShapeDtypeStruct(arrived.shape...  1.7 us
    pallas_call x1, Pallas kernels, prepare(): pl.pallas_call(prepare_kernel, out_shape=[paired, paired, jax.ShapeDtypeS...  1.28 us
  transfers between devices with their start and end apart: 3, of which 2 were waited for; matrix products, arithmetic and copies ran while one was open for 0% of the time, Pallas kernels for 11%

profile of v4, /device:TPU:1, one launch (start us, length us, event | category | flops | bytes accessed | tf_op | source)
XLA Modules:
  0.0 58.8 jit_solution(1593283138296243965)
XLA Ops:
  0.0 0.0 copy-start.1
  0.0 1.9 %pack.1 = bf16[1152,128]{1,0:T(8,128)(2,1)} custom-call(s32[8,16]{1,0:T(8,128)} %prefix_hbm.3, bf16[8,1024]{1,0:T(8,128)(2,1)} %queries_hbm.3), custom_call_target="tpu_custom_call" | custom-call | flops 4194304 | bytes 524288 | tf_op jit(solution)/shard_map/pack/pallas_call | solution.py:104
  1.9 18.5 %all-to-all-start = ((bf16[64,9,2,128]{3,2,1,0:T(2,128)(2,1)}), bf16[64,9,2,128]{3,2,1,0:T(2,128)(2,1)S(1)}, u32[]{:S(2)}, u32[]{:S(2)}) async-start(bf16[64,9,2,128]{3,2,1,0:T(2,128)(2,1)} %bitcast.1), calls=%async_computation | async-start | bytes 589824 | tf_op jit(solution)/shard_map/all_to_all | solution.py:445
  21.1 1.3 %prepare.1 = (bf16[512,256]{1,0:T(8,128)(2,1)S(1)}, bf16[512,256]{1,0:T(8,128)(2,1)S(1)}, bf16[1040,256]{1,0:T(8,128)(2,1)S(1)}) custom-call(s32[1]{0:T(128)S(6)} %copy.8.mig, s32[8]{0:T(128)} %lengths.1, bf16[1024,256]{1,0:T(8,128)(2,1)} %bitcast.9, bf16[8,1024,256]{2,1,0:T(8,128)(2,1)} %cache_hbm.1), custom_call_target="tpu_custom_call" | custom-call | bytes 1048576 | tf_op jit(solution)/shard_map/prepare/pallas_call | solution.py:169
  22.4 3.3 %collective-permute-start = (bf16[1040,256]{1,0:T(8,128)(2,1)S(1)}, bf16[1040,256]{1,0:T(8,128)(2,1)S(1)}, u32[]{:S(2)}, u32[]{:S(2)}) collective-permute-start(bf16[1040,256]{1,0:T(8,128)(2,1)S(1)} %get-tuple-element.10), channel_id=1, source_target_pairs={{0,256},{8,264},{16,272},{24,280},{32,288},{40,296},{48,304},{56,3... | collective-permute-start | bytes 1597448 | tf_op jit(solution)/shard_map/ppermute | solution.py:452
  25.7 1.8 %all-to-all-done = bf16[64,9,2,128]{3,2,1,0:T(2,128)(2,1)S(1)} async-done(((bf16[64,9,2,128]{3,2,1,0:T(2,128)(2,1)}), bf16[64,9,2,128]{3,2,1,0:T(2,128)(2,1)S(1)}, u32[]{:S(2)}, u32[]{:S(2)}) %all-to-all-start) | async-done | bytes 294944 | tf_op jit(solution)/shard_map/all_to_all | solution.py:445
  27.4 1.7 %owner.1 = bf16[1152,128]{1,0:T(8,128)(2,1)} custom-call(bf16[1152,128]{1,0:T(8,128)(2,1)S(1)} %bitcast.7, bf16[512,256]{1,0:T(8,128)(2,1)S(1)} %get-tuple-element.12.keys, bf16[512,256]{1,0:T(8,128)(2,1)S(1)} %get-tuple-element.13.values), custom_call_target="tpu_custom_call" | custom-call | flops 536870912 | bytes 2097152 | tf_op jit(solution)/shard_map/owner/pallas_call | solution.py:352
  29.1 11.3 %all-to-all-start.1 = ((bf16[64,9,2,128]{3,2,1,0:T(2,128)(2,1)}), bf16[64,9,2,128]{3,2,1,0:T(2,128)(2,1)S(1)}, u32[]{:S(2)}, u32[]{:S(2)}) async-start(bf16[64,9,2,128]{3,2,1,0:T(2,128)(2,1)} %bitcast.3), calls=%async_computation.1 | async-start | bytes 589824 | tf_op jit(solution)/shard_map/all_to_all | solution.py:445
  40.4 0.0 copy-start
  40.4 0.0 collective-permute-done.moved
  40.4 0.0 copy-done.1
  40.4 3.3 %resident.1 = (f32[8,16,128]{2,1,0:T(8,128)S(1)}, s32[8,128]{1,0:T(8,128)S(1)}) custom-call(s32[1]{0:T(128)S(6)} %copy.8.mig, s32[8]{0:T(128)S(1)} %copy-done.1, bf16[8,1024]{1,0:T(8,128)(2,1)} %queries_hbm.3, bf16[8,256]{1,0:T(8,128)(2,1)} %new_kv.1, s32[8,16]{1,0:T(8,128)} %prefix_hbm.3, bf16[1040,256]{1,0:T(8,128)(2,1)S(1)} %collective-permute-done.moved, ...), custom_call_target="tpu_custom_call" | custom-call | flops 17179869184 | bytes 67108864 | tf_op jit(solution)/shard_map/resident/pallas_call | solution.py:253
  43.8 3.7 %all-to-all-done.1 = bf16[64,9,2,128]{3,2,1,0:T(2,128)(2,1)S(1)} async-done(((bf16[64,9,2,128]{3,2,1,0:T(2,128)(2,1)}), bf16[64,9,2,128]{3,2,1,0:T(2,128)(2,1)S(1)}, u32[]{:S(2)}, u32[]{:S(2)}) %all-to-all-start.1) | async-done | bytes 294944 | tf_op jit(solution)/shard_map/all_to_all | solution.py:445
  47.4 0.0 copy-done
  47.4 0.5 combine.1
  48.0 10.2 %all_to_all.15 = bf16[8,8,128]{2,1,0:T(8,128)(2,1)S(1)} all-to-all(bf16[8,8,128]{2,1,0:T(8,128)(2,1)S(1)} %bitcast.8), channel_id=1, replica_groups={{4,5,6,7,0,1,2,3},{12,13,14,15,8,9,10,11},{20,21,22,23,16,17,18,19},{28..., dimensions={0} | all-to-all | bytes 32768 | tf_op jit(solution)/shard_map/all_to_all | solution.py:459
  58.2 0.6 %reshape.27 = bf16[1,8192]{1,0:T(2,128)(2,1)} reshape(bf16[8,8,128]{2,1,0:T(8,128)(2,1)S(1)} %pad_maximum_fusion) | data formatting | bytes 32768 | tf_op jit(solution)/shard_map/reshape | solution.py:463
  (2 shorter events, 0.0 us)
Async XLA Ops:
  0.0 40.4 %copy-start.1 = (s32[8]{0:T(128)S(1)}, s32[8]{0:T(128)}, u32[]{:S(2)}) copy-start(s32[8]{0:T(128)} %lengths.1) | copy-start | bytes 100
  1.9 25.6 %all-to-all-start = ((bf16[64,9,2,128]{3,2,1,0:T(2,128)(2,1)}), bf16[64,9,2,128]{3,2,1,0:T(2,128)(2,1)S(1)}, u32[]{:S(2)}, u32[]{:S(2)}) async-start(bf16[64,9,2,128]{3,2,1,0:T(2,128)(2,1)} %bitcast.1), calls=%async_computation | async-start | bytes 589824 | tf_op jit(solution)/shard_map/all_to_all | solution.py:445
  22.4 18.1 %collective-permute-start = (bf16[1040,256]{1,0:T(8,128)(2,1)S(1)}, bf16[1040,256]{1,0:T(8,128)(2,1)S(1)}, u32[]{:S(2)}, u32[]{:S(2)}) collective-permute-start(bf16[1040,256]{1,0:T(8,128)(2,1)S(1)} %get-tuple-element.10), channel_id=1, source_target_pairs={{0,256},{8,264},{16,272},{24,280},{32,288},{40,296},{48,304},{56,3... | collective-permute-start | bytes 1597448 | tf_op jit(solution)/shard_map/ppermute | solution.py:452
  29.1 18.3 %all-to-all-start.1 = ((bf16[64,9,2,128]{3,2,1,0:T(2,128)(2,1)}), bf16[64,9,2,128]{3,2,1,0:T(2,128)(2,1)S(1)}, u32[]{:S(2)}, u32[]{:S(2)}) async-start(bf16[64,9,2,128]{3,2,1,0:T(2,128)(2,1)} %bitcast.3), calls=%async_computation.1 | async-start | bytes 589824 | tf_op jit(solution)/shard_map/all_to_all | solution.py:445
  40.4 7.0 %copy-start = (bf16[8,256]{1,0:T(8,128)(2,1)S(1)}, bf16[8,256]{1,0:T(8,128)(2,1)}, u32[]{:S(2)}) copy-start(bf16[8,256]{1,0:T(8,128)(2,1)} %new_kv.1) | copy-start | bytes 12292

commit v5 on v4

--- a/solution.py
+++ b/solution.py
@@ -12,7 +12,7 @@
 GRP = QH // KVH
 CAP = 2
 NONE = 8191
-FIRST = 20
+LEAD_X, LEAD_Z = 2, 4
 FIRST_TP = 4
 TAIL = 16
 HEADS = 4
@@ -39,10 +39,21 @@
     return lax.broadcasted_iota(jnp.int32, shape, len(shape) - 1)
 
 
+def step(n):
+    half = (n + 1) >> 1
+    return half * (2 * (n & 1) - 1)
+
+
+def member(r):
+    z = (LEAD_Z + step(r >> 3)) & 7
+    x = (LEAD_X + step((r >> 1) & 3)) & 3
+    return ((r & 1) * 4 + x) * 8 + z
+
+
 def slot_codes(ids, insts):
     rows, width = ids.shape
     slots = CAP * insts
-    lane = (lanes((rows, slots)) & (insts - 1)) ^ FIRST
+    lane = member(lanes((rows, slots)) & (insts - 1))
     row = lax.broadcasted_iota(jnp.int32, (rows, slots), 0)
     first = jnp.full((rows, slots), NONE, jnp.int32)
     last = jnp.full((rows, slots), -1, jnp.int32)
@@ -437,7 +448,7 @@
     rows = queries.shape[0]
     insts = lax.axis_size("inst")
     swap = [(i, i ^ (insts // 2)) for i in range(insts)]
-    order = [[r ^ FIRST for r in range(insts)]]
+    order = [[member(r) for r in range(insts)]]
     order_tp = [[r ^ FIRST_TP for r in range(rows)]]
 
     def exchange(messages):

time: 59.2 us -> 59.6 us (level)
  no operation moved by 1% of the time
where the time goes in v5:
time: 59.6 us; the launch traced here: 59.2 us
  starting transfers between devices  33.5 us (56%)
  blocking collectives  9.97 us (17%)
  Pallas kernels  8.71 us (15%)
  waiting for transfers between devices  5.7 us (10%)
  between operations  0.74 us (1%)
  local copies, waits for them, and re-layouts  0.64 us (1%)
    all_to_all x2, starting transfers between devices, exchange(): lax.all_to_all(messages, 'inst', split_axis=0, concat_axis=0, axis_index_...  30.4 us
    all_to_all x1, blocking collectives, on_device(): lax.all_to_all(attended, 'tp', split_axis=0, concat_axis=0, axis_index_gr...  9.97 us
    all_to_all x2, waiting for transfers between devices, exchange(): lax.all_to_all(messages, 'inst', split_axis=0, concat_axis=0, axis_index_...  5.7 us
    pallas_call x1, Pallas kernels, resident(): pl.pallas_call(resident_kernel, out_shape=[jax.ShapeDtypeStruct((rows, 2...  3.32 us
    ppermute x1, starting transfers between devices, on_device(): moved = lax.ppermute(leaving, 'inst', swap)  3.1 us
    pallas_call x1, Pallas kernels, pack(): pl.pallas_call(pack_kernel, out_shape=jax.ShapeDtypeStruct((size, HD), jn...  1.87 us
    pallas_call x1, Pallas kernels, owner(): pl.pallas_call(owner_kernel, out_shape=jax.ShapeDtypeStruct(arrived.shape...  1.71 us
    pallas_call x1, Pallas kernels, prepare(): pl.pallas_call(prepare_kernel, out_shape=[paired, paired, jax.ShapeDtypeS...  1.28 us
  transfers between devices with their start and end apart: 3, of which 2 were waited for; matrix products, arithmetic and copies ran while one was open for 0% of the time, Pallas kernels for 11%

profile of v5, /device:TPU:1, one launch (start us, length us, event | category | flops | bytes accessed | tf_op | source)
XLA Modules:
  0.0 59.2 jit_solution(11171389452307952310)
XLA Ops:
  0.0 0.0 copy-start.1
  0.0 1.9 %pack.1 = bf16[1152,128]{1,0:T(8,128)(2,1)} custom-call(s32[8,16]{1,0:T(8,128)} %prefix_hbm.3, bf16[8,1024]{1,0:T(8,128)(2,1)} %queries_hbm.3), custom_call_target="tpu_custom_call" | custom-call | flops 4194304 | bytes 524288 | tf_op jit(solution)/shard_map/pack/pallas_call | solution.py:115
  1.9 18.8 %all-to-all-start = ((bf16[64,9,2,128]{3,2,1,0:T(2,128)(2,1)}), bf16[64,9,2,128]{3,2,1,0:T(2,128)(2,1)S(1)}, u32[]{:S(2)}, u32[]{:S(2)}) async-start(bf16[64,9,2,128]{3,2,1,0:T(2,128)(2,1)} %bitcast.1), calls=%async_computation | async-start | bytes 589824 | tf_op jit(solution)/shard_map/all_to_all | solution.py:456
  21.4 1.3 %prepare.1 = (bf16[512,256]{1,0:T(8,128)(2,1)S(1)}, bf16[512,256]{1,0:T(8,128)(2,1)S(1)}, bf16[1040,256]{1,0:T(8,128)(2,1)S(1)}) custom-call(s32[1]{0:T(128)S(6)} %copy.8.mig, s32[8]{0:T(128)} %lengths.1, bf16[1024,256]{1,0:T(8,128)(2,1)} %bitcast.9, bf16[8,1024,256]{2,1,0:T(8,128)(2,1)} %cache_hbm.1), custom_call_target="tpu_custom_call" | custom-call | bytes 1048576 | tf_op jit(solution)/shard_map/prepare/pallas_call | solution.py:180
  22.6 3.1 %collective-permute-start = (bf16[1040,256]{1,0:T(8,128)(2,1)S(1)}, bf16[1040,256]{1,0:T(8,128)(2,1)S(1)}, u32[]{:S(2)}, u32[]{:S(2)}) collective-permute-start(bf16[1040,256]{1,0:T(8,128)(2,1)S(1)} %get-tuple-element.10), channel_id=1, source_target_pairs={{0,256},{8,264},{16,272},{24,280},{32,288},{40,296},{48,304},{56,3... | collective-permute-start | bytes 1597448 | tf_op jit(solution)/shard_map/ppermute | solution.py:463
  25.7 2.0 %all-to-all-done = bf16[64,9,2,128]{3,2,1,0:T(2,128)(2,1)S(1)} async-done(((bf16[64,9,2,128]{3,2,1,0:T(2,128)(2,1)}), bf16[64,9,2,128]{3,2,1,0:T(2,128)(2,1)S(1)}, u32[]{:S(2)}, u32[]{:S(2)}) %all-to-all-start) | async-done | bytes 294944 | tf_op jit(solution)/shard_map/all_to_all | solution.py:456
  27.7 1.7 %owner.1 = bf16[1152,128]{1,0:T(8,128)(2,1)} custom-call(bf16[1152,128]{1,0:T(8,128)(2,1)S(1)} %bitcast.7, bf16[512,256]{1,0:T(8,128)(2,1)S(1)} %get-tuple-element.12.keys, bf16[512,256]{1,0:T(8,128)(2,1)S(1)} %get-tuple-element.13.values), custom_call_target="tpu_custom_call" | custom-call | flops 536870912 | bytes 2097152 | tf_op jit(solution)/shard_map/owner/pallas_call | solution.py:363
  29.4 11.6 %all-to-all-start.1 = ((bf16[64,9,2,128]{3,2,1,0:T(2,128)(2,1)}), bf16[64,9,2,128]{3,2,1,0:T(2,128)(2,1)S(1)}, u32[]{:S(2)}, u32[]{:S(2)}) async-start(bf16[64,9,2,128]{3,2,1,0:T(2,128)(2,1)} %bitcast.3), calls=%async_computation.1 | async-start | bytes 589824 | tf_op jit(solution)/shard_map/all_to_all | solution.py:456
  41.0 0.0 copy-start
  41.0 0.0 collective-permute-done.moved
  41.0 0.0 copy-done.1
  41.0 3.3 %resident.1 = (f32[8,16,128]{2,1,0:T(8,128)S(1)}, s32[8,128]{1,0:T(8,128)S(1)}) custom-call(s32[1]{0:T(128)S(6)} %copy.8.mig, s32[8]{0:T(128)S(1)} %copy-done.1, bf16[8,1024]{1,0:T(8,128)(2,1)} %queries_hbm.3, bf16[8,256]{1,0:T(8,128)(2,1)} %new_kv.1, s32[8,16]{1,0:T(8,128)} %prefix_hbm.3, bf16[1040,256]{1,0:T(8,128)(2,1)S(1)} %collective-permute-done.moved, ...), custom_call_target="tpu_custom_call" | custom-call | flops 17179869184 | bytes 67108864 | tf_op jit(solution)/shard_map/resident/pallas_call | solution.py:264
  44.4 3.7 %all-to-all-done.1 = bf16[64,9,2,128]{3,2,1,0:T(2,128)(2,1)S(1)} async-done(((bf16[64,9,2,128]{3,2,1,0:T(2,128)(2,1)}), bf16[64,9,2,128]{3,2,1,0:T(2,128)(2,1)S(1)}, u32[]{:S(2)}, u32[]{:S(2)}) %all-to-all-start.1) | async-done | bytes 294944 | tf_op jit(solution)/shard_map/all_to_all | solution.py:456
  48.1 0.0 copy-done
  48.1 0.5 combine.1
  48.6 10.0 %all_to_all.15 = bf16[8,8,128]{2,1,0:T(8,128)(2,1)S(1)} all-to-all(bf16[8,8,128]{2,1,0:T(8,128)(2,1)S(1)} %bitcast.8), channel_id=1, replica_groups={{4,5,6,7,0,1,2,3},{12,13,14,15,8,9,10,11},{20,21,22,23,16,17,18,19},{28..., dimensions={0} | all-to-all | bytes 32768 | tf_op jit(solution)/shard_map/all_to_all | solution.py:470
  58.6 0.6 %reshape.27 = bf16[1,8192]{1,0:T(2,128)(2,1)} reshape(bf16[8,8,128]{2,1,0:T(8,128)(2,1)S(1)} %pad_maximum_fusion) | data formatting | bytes 32768 | tf_op jit(solution)/shard_map/reshape | solution.py:474
  (2 shorter events, 0.0 us)
Async XLA Ops:
  0.0 41.0 %copy-start.1 = (s32[8]{0:T(128)S(1)}, s32[8]{0:T(128)}, u32[]{:S(2)}) copy-start(s32[8]{0:T(128)} %lengths.1) | copy-start | bytes 100
  1.9 25.8 %all-to-all-start = ((bf16[64,9,2,128]{3,2,1,0:T(2,128)(2,1)}), bf16[64,9,2,128]{3,2,1,0:T(2,128)(2,1)S(1)}, u32[]{:S(2)}, u32[]{:S(2)}) async-start(bf16[64,9,2,128]{3,2,1,0:T(2,128)(2,1)} %bitcast.1), calls=%async_computation | async-start | bytes 589824 | tf_op jit(solution)/shard_map/all_to_all | solution.py:456
  22.6 18.4 %collective-permute-start = (bf16[1040,256]{1,0:T(8,128)(2,1)S(1)}, bf16[1040,256]{1,0:T(8,128)(2,1)S(1)}, u32[]{:S(2)}, u32[]{:S(2)}) collective-permute-start(bf16[1040,256]{1,0:T(8,128)(2,1)S(1)} %get-tuple-element.10), channel_id=1, source_target_pairs={{0,256},{8,264},{16,272},{24,280},{32,288},{40,296},{48,304},{56,3... | collective-permute-start | bytes 1597448 | tf_op jit(solution)/shard_map/ppermute | solution.py:463
  29.4 18.7 %all-to-all-start.1 = ((bf16[64,9,2,128]{3,2,1,0:T(2,128)(2,1)}), bf16[64,9,2,128]{3,2,1,0:T(2,128)(2,1)S(1)}, u32[]{:S(2)}, u32[]{:S(2)}) async-start(bf16[64,9,2,128]{3,2,1,0:T(2,128)(2,1)} %bitcast.3), calls=%async_computation.1 | async-start | bytes 589824 | tf_op jit(solution)/shard_map/all_to_all | solution.py:456
  41.0 7.1 %copy-start = (bf16[8,256]{1,0:T(8,128)(2,1)S(1)}, bf16[8,256]{1,0:T(8,128)(2,1)}, u32[]{:S(2)}) copy-start(bf16[8,256]{1,0:T(8,128)(2,1)} %new_kv.1) | copy-start | bytes 12292

commit v6 on v4

--- a/solution.py
+++ b/solution.py
@@ -12,7 +12,7 @@
 GRP = QH // KVH
 CAP = 2
 NONE = 8191
-FIRST = 20
+FIRST = 21
 FIRST_TP = 4
 TAIL = 16
 HEADS = 4

time: 59.2 us -> 59.5 us (level)
  starting transfers between devices: 33.1 us -> 32 us
  blocking collectives: 10.2 us -> 11 us
    all_to_all x2, starting transfers between devices: 29.8 us -> 28.7 us  [exchange(): lax.all_to_all(messages, 'inst', split_axis=0, concat_axis=0, axis_index_...]
    all_to_all x1, blocking collectives: 10.2 us -> 11 us  [on_device(): lax.all_to_all(attended, 'tp', split_axis=0, concat_axis=0, axis_index_gr...]
where the time goes in v6:
time: 59.5 us; the launch traced here: 59.1 us
  starting transfers between devices  32 us (54%)
  blocking collectives  11 us (18%)
  Pallas kernels  8.72 us (15%)
  waiting for transfers between devices  5.99 us (10%)
  between operations  0.74 us (1%)
  local copies, waits for them, and re-layouts  0.64 us (1%)
    all_to_all x2, starting transfers between devices, exchange(): lax.all_to_all(messages, 'inst', split_axis=0, concat_axis=0, axis_index_...  28.7 us
    all_to_all x1, blocking collectives, on_device(): lax.all_to_all(attended, 'tp', split_axis=0, concat_axis=0, axis_index_gr...  11 us
    all_to_all x2, waiting for transfers between devices, exchange(): lax.all_to_all(messages, 'inst', split_axis=0, concat_axis=0, axis_index_...  5.99 us
    pallas_call x1, Pallas kernels, resident(): pl.pallas_call(resident_kernel, out_shape=[jax.ShapeDtypeStruct((rows, 2...  3.33 us
    ppermute x1, starting transfers between devices, on_device(): moved = lax.ppermute(leaving, 'inst', swap)  3.31 us
    pallas_call x1, Pallas kernels, pack(): pl.pallas_call(pack_kernel, out_shape=jax.ShapeDtypeStruct((size, HD), jn...  1.87 us
    pallas_call x1, Pallas kernels, owner(): pl.pallas_call(owner_kernel, out_shape=jax.ShapeDtypeStruct(arrived.shape...  1.71 us
    pallas_call x1, Pallas kernels, prepare(): pl.pallas_call(prepare_kernel, out_shape=[paired, paired, jax.ShapeDtypeS...  1.28 us
  transfers between devices with their start and end apart: 3, of which 2 were waited for; matrix products, arithmetic and copies ran while one was open for 0% of the time, Pallas kernels for 11%

profile of v6, /device:TPU:1, one launch (start us, length us, event | category | flops | bytes accessed | tf_op | source)
XLA Modules:
  0.0 59.1 jit_solution(9573800227381623923)
XLA Ops:
  0.0 0.0 copy-start.1
  0.0 1.9 %pack.1 = bf16[1152,128]{1,0:T(8,128)(2,1)} custom-call(s32[8,16]{1,0:T(8,128)} %prefix_hbm.3, bf16[8,1024]{1,0:T(8,128)(2,1)} %queries_hbm.3), custom_call_target="tpu_custom_call" | custom-call | flops 4194304 | bytes 524288 | tf_op jit(solution)/shard_map/pack/pallas_call | solution.py:104
  1.9 17.6 %all-to-all-start = ((bf16[64,9,2,128]{3,2,1,0:T(2,128)(2,1)}), bf16[64,9,2,128]{3,2,1,0:T(2,128)(2,1)S(1)}, u32[]{:S(2)}, u32[]{:S(2)}) async-start(bf16[64,9,2,128]{3,2,1,0:T(2,128)(2,1)} %bitcast.1), calls=%async_computation | async-start | bytes 589824 | tf_op jit(solution)/shard_map/all_to_all | solution.py:445
  20.2 1.3 %prepare.1 = (bf16[512,256]{1,0:T(8,128)(2,1)S(1)}, bf16[512,256]{1,0:T(8,128)(2,1)S(1)}, bf16[1040,256]{1,0:T(8,128)(2,1)S(1)}) custom-call(s32[1]{0:T(128)S(6)} %copy.8.mig, s32[8]{0:T(128)} %lengths.1, bf16[1024,256]{1,0:T(8,128)(2,1)} %bitcast.9, bf16[8,1024,256]{2,1,0:T(8,128)(2,1)} %cache_hbm.1), custom_call_target="tpu_custom_call" | custom-call | bytes 1048576 | tf_op jit(solution)/shard_map/prepare/pallas_call | solution.py:169
  21.5 3.3 %collective-permute-start = (bf16[1040,256]{1,0:T(8,128)(2,1)S(1)}, bf16[1040,256]{1,0:T(8,128)(2,1)S(1)}, u32[]{:S(2)}, u32[]{:S(2)}) collective-permute-start(bf16[1040,256]{1,0:T(8,128)(2,1)S(1)} %get-tuple-element.10), channel_id=1, source_target_pairs={{0,256},{8,264},{16,272},{24,280},{32,288},{40,296},{48,304},{56,3... | collective-permute-start | bytes 1597448 | tf_op jit(solution)/shard_map/ppermute | solution.py:452
  24.8 2.1 %all-to-all-done = bf16[64,9,2,128]{3,2,1,0:T(2,128)(2,1)S(1)} async-done(((bf16[64,9,2,128]{3,2,1,0:T(2,128)(2,1)}), bf16[64,9,2,128]{3,2,1,0:T(2,128)(2,1)S(1)}, u32[]{:S(2)}, u32[]{:S(2)}) %all-to-all-start) | async-done | bytes 294944 | tf_op jit(solution)/shard_map/all_to_all | solution.py:445
  26.9 1.7 %owner.1 = bf16[1152,128]{1,0:T(8,128)(2,1)} custom-call(bf16[1152,128]{1,0:T(8,128)(2,1)S(1)} %bitcast.7, bf16[512,256]{1,0:T(8,128)(2,1)S(1)} %get-tuple-element.12.keys, bf16[512,256]{1,0:T(8,128)(2,1)S(1)} %get-tuple-element.13.values), custom_call_target="tpu_custom_call" | custom-call | flops 536870912 | bytes 2097152 | tf_op jit(solution)/shard_map/owner/pallas_call | solution.py:352
  28.6 11.1 %all-to-all-start.1 = ((bf16[64,9,2,128]{3,2,1,0:T(2,128)(2,1)}), bf16[64,9,2,128]{3,2,1,0:T(2,128)(2,1)S(1)}, u32[]{:S(2)}, u32[]{:S(2)}) async-start(bf16[64,9,2,128]{3,2,1,0:T(2,128)(2,1)} %bitcast.3), calls=%async_computation.1 | async-start | bytes 589824 | tf_op jit(solution)/shard_map/all_to_all | solution.py:445
  39.7 0.0 copy-start
  39.7 0.0 collective-permute-done.moved
  39.7 0.0 copy-done.1
  39.7 3.3 %resident.1 = (f32[8,16,128]{2,1,0:T(8,128)S(1)}, s32[8,128]{1,0:T(8,128)S(1)}) custom-call(s32[1]{0:T(128)S(6)} %copy.8.mig, s32[8]{0:T(128)S(1)} %copy-done.1, bf16[8,1024]{1,0:T(8,128)(2,1)} %queries_hbm.3, bf16[8,256]{1,0:T(8,128)(2,1)} %new_kv.1, s32[8,16]{1,0:T(8,128)} %prefix_hbm.3, bf16[1040,256]{1,0:T(8,128)(2,1)S(1)} %collective-permute-done.moved, ...), custom_call_target="tpu_custom_call" | custom-call | flops 17179869184 | bytes 67108864 | tf_op jit(solution)/shard_map/resident/pallas_call | solution.py:253
  43.1 3.9 %all-to-all-done.1 = bf16[64,9,2,128]{3,2,1,0:T(2,128)(2,1)S(1)} async-done(((bf16[64,9,2,128]{3,2,1,0:T(2,128)(2,1)}), bf16[64,9,2,128]{3,2,1,0:T(2,128)(2,1)S(1)}, u32[]{:S(2)}, u32[]{:S(2)}) %all-to-all-start.1) | async-done | bytes 294944 | tf_op jit(solution)/shard_map/all_to_all | solution.py:445
  46.9 0.0 copy-done
  46.9 0.5 combine.1
  47.5 11.0 %all_to_all.15 = bf16[8,8,128]{2,1,0:T(8,128)(2,1)S(1)} all-to-all(bf16[8,8,128]{2,1,0:T(8,128)(2,1)S(1)} %bitcast.8), channel_id=1, replica_groups={{4,5,6,7,0,1,2,3},{12,13,14,15,8,9,10,11},{20,21,22,23,16,17,18,19},{28..., dimensions={0} | all-to-all | bytes 32768 | tf_op jit(solution)/shard_map/all_to_all | solution.py:459
  58.5 0.6 %reshape.27 = bf16[1,8192]{1,0:T(2,128)(2,1)} reshape(bf16[8,8,128]{2,1,0:T(8,128)(2,1)S(1)} %pad_maximum_fusion) | data formatting | bytes 32768 | tf_op jit(solution)/shard_map/reshape | solution.py:463
  (2 shorter events, 0.0 us)
Async XLA Ops:
  0.0 39.7 %copy-start.1 = (s32[8]{0:T(128)S(1)}, s32[8]{0:T(128)}, u32[]{:S(2)}) copy-start(s32[8]{0:T(128)} %lengths.1) | copy-start | bytes 100
  1.9 25.0 %all-to-all-start = ((bf16[64,9,2,128]{3,2,1,0:T(2,128)(2,1)}), bf16[64,9,2,128]{3,2,1,0:T(2,128)(2,1)S(1)}, u32[]{:S(2)}, u32[]{:S(2)}) async-start(bf16[64,9,2,128]{3,2,1,0:T(2,128)(2,1)} %bitcast.1), calls=%async_computation | async-start | bytes 589824 | tf_op jit(solution)/shard_map/all_to_all | solution.py:445
  21.5 18.3 %collective-permute-start = (bf16[1040,256]{1,0:T(8,128)(2,1)S(1)}, bf16[1040,256]{1,0:T(8,128)(2,1)S(1)}, u32[]{:S(2)}, u32[]{:S(2)}) collective-permute-start(bf16[1040,256]{1,0:T(8,128)(2,1)S(1)} %get-tuple-element.10), channel_id=1, source_target_pairs={{0,256},{8,264},{16,272},{24,280},{32,288},{40,296},{48,304},{56,3... | collective-permute-start | bytes 1597448 | tf_op jit(solution)/shard_map/ppermute | solution.py:452
  28.6 18.3 %all-to-all-start.1 = ((bf16[64,9,2,128]{3,2,1,0:T(2,128)(2,1)}), bf16[64,9,2,128]{3,2,1,0:T(2,128)(2,1)S(1)}, u32[]{:S(2)}, u32[]{:S(2)}) async-start(bf16[64,9,2,128]{3,2,1,0:T(2,128)(2,1)} %bitcast.3), calls=%async_computation.1 | async-start | bytes 589824 | tf_op jit(solution)/shard_map/all_to_all | solution.py:445
  39.7 7.2 %copy-start = (bf16[8,256]{1,0:T(8,128)(2,1)S(1)}, bf16[8,256]{1,0:T(8,128)(2,1)}, u32[]{:S(2)}) copy-start(bf16[8,256]{1,0:T(8,128)(2,1)} %new_kv.1) | copy-start | bytes 12292
